TPU v7x, 512 devices: a whole 4x4x16 slice. The times are simulated.
512 devices in a mesh: dp: 64 (over z, y), tensor: 8 (over x, core).
Axes of the slice: x: 4, y: 4, z: 16, core: 2. Of those that a mesh axis runs over, the one named last changes fastest.
Arguments:
- grads: bfloat16 [131072, 3072], P('dp', 'tensor'), may hold values from -16 to 16, as said below
- errors: bfloat16 [131072, 3072], P('dp', 'tensor'), may hold values from -4 to 4
- q_init: float32 [3072, 128], P('tensor'), may hold values from -6 to 6
Outputs:
- avg_grad: bfloat16 [2048, 3072], P('dp', 'tensor')
- new_errors: bfloat16 [131072, 3072], P('dp', 'tensor')
- q_next: float32 [3072, 128], P('tensor')
Inputs may be any that keep to these rules, and one draw needn't show every extreme that they name: `grads`: gradients of the 64 replicas, stacked along rows.
All inputs are finite; a program needn't handle non-finite values.
Results may differ from a plain program's by a relative error of at most 0.0035.
Values sent between devices are 32-bit elements; how exact they have to be, the bound alone decides.
No kernel may reach another device: no remote copies, remote signals or barrier semaphores. Data moves between devices by JAX's collectives and lax.ppermute only.
A program may use at most 64 MiB of HBM per device.

v0:
```python
import jax
import jax.numpy as jnp
from jax import lax
from jax.sharding import PartitionSpec as P


def cholesky_qr(values, reducer):
    for sweep in range(2):
        gram_local = lax.dot_general(
            values, values, (((0,), (0,)), ((), ())), precision=lax.Precision.HIGHEST
        )
        gram_total = reducer(gram_local)
        lower = jnp.linalg.cholesky(gram_total)
        values = jax.scipy.linalg.solve_triangular(lower, values.T, lower=True).T
    return values


def body(grads, errors, q_init):
    merged = grads.astype(jnp.float32) + errors.astype(jnp.float32)
    replicas = lax.axis_size("dp")
    share_rows = merged.shape[0] // replicas
    power_part = jnp.dot(merged, q_init, precision=lax.Precision.HIGHEST)
    power_total = lax.psum(power_part, ("dp", "tensor"))
    ortho_basis = cholesky_qr(power_total, lambda gram_local: gram_local)
    q_terms = lax.dot_general(
        merged, ortho_basis, (((0,), (0,)), ((), ())), precision=lax.Precision.HIGHEST
    )
    factor_q = lax.psum(q_terms, "dp") * (1.0 / replicas)
    approx = lax.dot_general(
        ortho_basis, factor_q, (((1,), (1,)), ((), ())), precision=lax.Precision.HIGHEST
    )
    new_errors = (merged - approx).astype(jnp.bfloat16)
    own_start = lax.axis_index("dp") * share_rows
    own_rows = lax.dynamic_slice_in_dim(approx, own_start, share_rows, 0)
    return (own_rows.astype(jnp.bfloat16), new_errors, factor_q)


def solution(mesh):
    placed = (P("dp", "tensor"), P("dp", "tensor"), P("tensor", None))
    return jax.shard_map(
        body,
        mesh=mesh,
        in_specs=placed,
        out_specs=(P("dp", "tensor"), P("dp", "tensor"), P("tensor", None)),
        check_vma=False,
    )
```

profile of v0, /device:TPU:4, one launch (start us, length us, event | category | flops | bytes accessed | tf_op | source)
XLA Modules:
  0.0 819.9 jit_solution(226212136327445191)
XLA Ops:
  7.2 0.0 copy-start
  7.2 0.0 all-reduce.3.cloned.1.call-start
  7.2 0.9 copy-done
  8.1 5.8 fusion.1
  13.9 0.0 all-reduce.3.cloned.1.call-update
  13.9 0.2 all-reduce.5.cloned.1.call-start
  14.1 470.8 %all-reduce.3.cloned.1.call-done = f32[2048,128]{1,0:T(8,128)} async-done(((f32[2048,128]{1,0:T(8,128)}), f32[2048,128]{1,0:T(8,128)}) %all-reduce.3.cloned.1.call-update) | async-done | bytes 1048592 | tf_op jit(solution)/shard_map/psum | solution.py:23
  484.9 3.4 fusion.13
  488.4 0.1 copy.6
  488.5 11.7 %cholesky.44 = f32[128,128]{1,0:T(8,128)S(1)} custom-call(f32[128,128]{1,0:T(8,128)S(1)} %fusion.10), custom_call_target="Cholesky" | custom-call | tf_op jit(solution)/shard_map/jit(cholesky)/cholesky | solution.py:13
  500.2 0.6 compare_reduce_fusion.1
  500.9 0.7 fusion.4
  501.5 9.8 %custom-call.6 = f32[1,128,128]{1,2,0:T(8,128)S(1)} custom-call(f32[1,128,128]{2,1,0:T(8,128)S(1)} %fusion.4), custom_call_target="InvertDiagBlocksLowerTriangular" | custom-call | tf_op jit(solution)/shard_map/jit(_solve_triangular)/triangular_solve | solution.py:14
  511.4 1.1 fusion.2
  512.4 1.0 fusion.14
  513.4 0.0 copy-start.1
  513.4 0.1 copy.7
  513.6 11.9 %cholesky.55 = f32[128,128]{1,0:T(8,128)S(1)} custom-call(f32[128,128]{1,0:T(8,128)S(1)} %fusion.8), custom_call_target="Cholesky" | custom-call | tf_op jit(solution)/shard_map/jit(cholesky)/cholesky | solution.py:13
  525.5 0.6 compare_reduce_fusion
  526.1 0.7 fusion.5
  526.8 9.8 %custom-call.7 = f32[1,128,128]{1,2,0:T(8,128)S(1)} custom-call(f32[1,128,128]{2,1,0:T(8,128)S(1)} %fusion.5), custom_call_target="InvertDiagBlocksLowerTriangular" | custom-call | tf_op jit(solution)/shard_map/jit(_solve_triangular)/triangular_solve | solution.py:14
  536.6 1.1 fusion.6
  537.7 1.0 copy-done.3
  538.6 0.0 copy-done.1
  538.7 7.3 fusion
  546.0 0.0 all-reduce.5.cloned.1.call-update
  546.0 259.3 %all-reduce.5.cloned.1.call-done = f32[384,128]{1,0:T(8,128)} async-done(((f32[384,128]{1,0:T(8,128)}), f32[384,128]{1,0:T(8,128)}) %all-reduce.5.cloned.1.call-update) | async-done | bytes 196624 | tf_op jit(solution)/shard_map/psum | solution.py:28
  805.2 0.9 broadcast_multiply_fusion
  806.2 0.0 copy-done.2
  806.2 0.0 copy-start.5
  806.2 6.2 subtract_convert_fusion
  812.4 0.6 dynamic-slice_convert_fusion
  (9 shorter events, 0.1 us)
Async XLA Ops:
  7.2 0.9 copy-start
  7.2 477.7 %all-reduce.3.cloned.1.call-start = ((), (), s32[]{:S(2)}) async-start(), calls=%async_computation | async-start | bytes 2097152 | tf_op jit(solution)/shard_map/psum | solution.py:23
  13.9 791.4 %all-reduce.5.cloned.1.call-start = ((), (), s32[]{:S(2)}) async-start(), calls=%async_computation.1 | async-start | bytes 393216 | tf_op jit(solution)/shard_map/psum | solution.py:28
  484.9 26.4 %copy-start.4 = (f32[2048,128]{1,0:T(8,128)S(1)}, f32[2048,128]{1,0:T(8,128)}, u32[]{:S(2)}) copy-start(f32[2048,128]{1,0:T(8,128)} %all-reduce.3.cloned.1.call-done) | copy-start | bytes 3145732
  513.4 25.2 %copy-start.1 = (bf16[2048,384]{1,0:T(8,128)(2,1)S(1)}, bf16[2048,384]{1,0:T(8,128)(2,1)}, u32[]{:S(2)}) copy-start(bf16[2048,384]{1,0:T(8,128)(2,1)} %param.7) | copy-start | bytes 4718596
  537.7 1.0 copy-start.3
  538.7 267.5 %copy-start.2 = (bf16[2048,384]{1,0:T(8,128)(2,1)S(1)}, bf16[2048,384]{1,0:T(8,128)(2,1)}, u32[]{:S(2)}) copy-start(bf16[2048,384]{1,0:T(8,128)(2,1)} %param.6) | copy-start | bytes 4718596
  806.2 6.2 copy-start.5
Sparse Core Ops, SparseCore 0:
  14.0 470.8 all-reduce.2
  546.1 259.1 all-reduce.4
where the time goes:
time: 820 us
  waiting for transfers between devices  730 us (89%)
  other arithmetic  46.8 us (6%)
  matrix products  25.8 us (3%)
  between operations  14.2 us (2%)
    psum x1, waiting for transfers between devices, body(): power_total = lax.psum(power_part, ('dp', 'tensor'))  471 us
    psum x1, waiting for transfers between devices, body(): factor_q = lax.psum(q_terms, 'dp') * (1.0 / replicas)  259 us
    another operation x6, other arithmetic, cholesky_qr(): lower = jnp.linalg.cholesky(gram_total)  24.9 us
    another operation x4, other arithmetic, cholesky_qr(): values = jax.scipy.linalg.solve_triangular(lower, values.T, lower=True).T  20.9 us
  transfers between devices with their start and end apart: 2, of which 2 were waited for; matrix products, arithmetic and copies ran while one was open for 0% of the time, Pallas kernels for 0%

commit v1 on v0

v1 whole, which is shorter than its diff:
```python
import functools

import jax
import jax.numpy as jnp
from jax import lax
from jax.experimental import pallas as pl
from jax.experimental.pallas import tpu as pltpu
from jax.sharding import Mesh, PartitionSpec as P

F32 = jnp.float32
BF16 = jnp.bfloat16
HIGHEST = lax.Precision.HIGHEST
ROWS_BY_ROWS = (((0,), (0,)), ((), ()))
LANES_BY_LANES = (((1,), (1,)), ((), ()))
WIDTH = 8
TILE = 512
VMEM_BYTES = 40 << 20

DP = ("far", "near", "y")
TENSOR = ("x", "core")


def pieces(values, count):
    parts = []
    for _ in range(count):
        part = values.astype(BF16)
        parts.append(part)
        values = values - part.astype(F32)
    return parts


def whole(ref_shape):
    return pl.BlockSpec(ref_shape, lambda *_: (0,) * len(ref_shape))


def power_kernel(grads_ref, errors_ref, q_ref, power_ref, split_ref):
    rank = q_ref.shape[1]

    @pl.when(pl.program_id(0) == 0)
    def _():
        for k, part in enumerate(pieces(q_ref[...], 3)):
            split_ref[:, k * rank : (k + 1) * rank] = part

    products = jnp.dot(grads_ref[...], split_ref[...], preferred_element_type=F32)
    products += jnp.dot(errors_ref[...], split_ref[...], preferred_element_type=F32)
    power_ref[...] = products[:, :rank] + (products[:, rank : 2 * rank] + products[:, 2 * rank :])


def power_terms(grads, errors, q_init):
    rows, cols = grads.shape
    rank = q_init.shape[1]
    tiled = pl.BlockSpec((TILE, cols), lambda i: (i, 0))
    return pl.pallas_call(
        power_kernel,
        grid=(rows // TILE,),
        out_shape=jax.ShapeDtypeStruct((rows, rank), F32),
        in_specs=[tiled, tiled, whole((cols, rank))],
        out_specs=pl.BlockSpec((TILE, rank), lambda i: (i, 0)),
        scratch_shapes=[pltpu.VMEM((cols, 3 * rank), BF16)],
        compiler_params=pltpu.CompilerParams(vmem_limit_bytes=VMEM_BYTES),
    )(grads, errors, q_init)


def inverse_factor(gram, work_ref, inverse_ref):
    rank = gram.shape[0]
    lanes = lax.broadcasted_iota(jnp.int32, (WIDTH, rank), 1)
    subs = lax.broadcasted_iota(jnp.int32, (WIDTH, rank), 0)
    spread = lambda row: jnp.broadcast_to(row, (WIDTH, rank))
    work_ref[...] = gram
    for low in range(0, rank, WIDTH):
        own = work_ref[low : low + WIDTH, :]
        inside = (lanes >= low) & (lanes < low + WIDTH)
        columns = [spread(own[:, low + k : low + k + 1]) for k in range(WIDTH)]
        block = jnp.where(inside, (lanes - low == subs).astype(F32), own)
        forward = jnp.zeros((WIDTH, rank), F32)
        pivots = jnp.ones((WIDTH, rank), F32)
        reciprocals = jnp.zeros((WIDTH, rank), F32)
        for j in range(WIDTH):
            heads = [spread(column[j : j + 1, :]) for column in columns[j:]]
            row = spread(block[j : j + 1, :])
            forward = jnp.where(subs == j, row, forward)
            pivots = jnp.where(subs == j, heads[0], pivots)
            reciprocal = 1.0 / heads[0]
            reciprocals = jnp.where(subs == j, reciprocal, reciprocals)
            factor = jnp.where(subs == j, 0.0, columns[j] * reciprocal)
            for k in range(j + 1, WIDTH):
                columns[k] = columns[k] - factor * heads[k - j]
            block = block - factor * row
        inverse_ref[low : low + WIDTH, :] = jnp.where(lanes < low + WIDTH, forward * lax.rsqrt(pivots), 0.0)
        block = block * reciprocals
        solved = [spread(block[k : k + 1, :]) for k in range(WIDTH)]
        for at in range(low + WIDTH, rank, WIDTH):
            rest = work_ref[at : at + WIDTH, :]
            terms = [spread(rest[:, low + k : low + k + 1]) * solved[k] for k in range(WIDTH)]
            while len(terms) > 1:
                terms = [a + b for a, b in zip(terms[::2], terms[1::2], strict=True)]
            work_ref[at : at + WIDTH, :] = jnp.where(inside, 0.0, rest) - terms[0]


def basis_kernel(power_ref, basis_ref, inverse_ref, work_ref, step_ref):
    first = None
    source = power_ref
    for _ in range(2):
        gram = lax.dot_general(source[...], source[...], ROWS_BY_ROWS, precision=HIGHEST, preferred_element_type=F32)
        inverse_factor(gram, work_ref, step_ref)
        step = step_ref[...]
        basis_ref[...] = lax.dot_general(source[...], step, LANES_BY_LANES, precision=HIGHEST, preferred_element_type=F32)
        source = basis_ref
        first = step if first is None else jnp.dot(step, first, precision=HIGHEST, preferred_element_type=F32)
    inverse_ref[...] = first


def basis_of(power):
    rows, rank = power.shape
    in_vmem = pl.BlockSpec(memory_space=pltpu.VMEM)
    return pl.pallas_call(
        basis_kernel,
        out_shape=(jax.ShapeDtypeStruct((rows, rank), F32), jax.ShapeDtypeStruct((rank, rank), F32)),
        in_specs=[in_vmem],
        out_specs=(in_vmem, in_vmem),
        scratch_shapes=[pltpu.VMEM((rank, rank), F32)] * 2,
        compiler_params=pltpu.CompilerParams(vmem_limit_bytes=VMEM_BYTES),
    )(power)


def factor_kernel(grads_ref, errors_ref, power_ref, terms_ref, sum_ref):
    rank = power_ref.shape[1]
    split = jnp.concatenate(pieces(power_ref[...], 2), axis=1)
    products = lax.dot_general(split, grads_ref[...], ROWS_BY_ROWS, preferred_element_type=F32)
    products += lax.dot_general(split, errors_ref[...], ROWS_BY_ROWS, preferred_element_type=F32)

    @pl.when(pl.program_id(0) == 0)
    def _():
        sum_ref[...] = products

    @pl.when(pl.program_id(0) > 0)
    def _():
        sum_ref[...] += products

    terms_ref[...] = sum_ref[:rank, :] + sum_ref[rank:, :]


def factor_terms(grads, errors, power):
    rows, cols = grads.shape
    rank = power.shape[1]
    tiled = pl.BlockSpec((TILE, cols), lambda i: (i, 0))
    return pl.pallas_call(
        factor_kernel,
        grid=(rows // TILE,),
        out_shape=jax.ShapeDtypeStruct((rank, cols), F32),
        in_specs=[tiled, tiled, pl.BlockSpec((TILE, rank), lambda i: (i, 0))],
        out_specs=whole((rank, cols)),
        scratch_shapes=[pltpu.VMEM((2 * rank, cols), F32)],
        compiler_params=pltpu.CompilerParams(vmem_limit_bytes=VMEM_BYTES),
    )(grads, errors, power)


def output_kernel(replicas, own_ref, grads_ref, errors_ref, basis_ref, share_ref, inverse_ref, terms_ref,
                  avg_ref, new_ref, q_ref, split_ref):
    def decompressed(rows):
        high, low = pieces(rows, 2)
        return jnp.dot(jnp.concatenate([high, high, low], axis=1), split_ref[...], preferred_element_type=F32)

    @pl.when(pl.program_id(0) == 0)
    def _():
        factor = jnp.dot(inverse_ref[...], terms_ref[...], precision=HIGHEST, preferred_element_type=F32)
        factor = factor * (1.0 / replicas)
        q_ref[...] = factor.T
        high, low = pieces(factor, 2)
        split_ref[...] = jnp.concatenate([high, low, high], axis=0)
        avg_ref[...] = decompressed(share_ref[...]).astype(BF16)

    merged = grads_ref[...].astype(F32) + errors_ref[...].astype(F32)
    new_ref[...] = (merged - decompressed(basis_ref[...])).astype(BF16)


def outputs(grads, errors, basis, inverse, terms, replicas, own):
    rows, cols = grads.shape
    rank = basis.shape[1]
    share = rows // replicas
    tiled = pl.BlockSpec((TILE, cols), lambda i, own: (i, 0))
    return pl.pallas_call(
        functools.partial(output_kernel, replicas),
        grid_spec=pltpu.PrefetchScalarGridSpec(
            num_scalar_prefetch=1,
            grid=(rows // TILE,),
            in_specs=[
                tiled,
                tiled,
                pl.BlockSpec((TILE, rank), lambda i, own: (i, 0)),
                pl.BlockSpec((share, rank), lambda i, own: (own[0], 0)),
                whole((rank, rank)),
                whole((rank, cols)),
            ],
            out_specs=(whole((share, cols)), tiled, whole((cols, rank))),
            scratch_shapes=[pltpu.VMEM((3 * rank, cols), BF16)],
        ),
        out_shape=(
            jax.ShapeDtypeStruct((share, cols), BF16),
            jax.ShapeDtypeStruct((rows, cols), BF16),
            jax.ShapeDtypeStruct((cols, rank), F32),
        ),
        compiler_params=pltpu.CompilerParams(vmem_limit_bytes=VMEM_BYTES),
    )(own, grads, errors, basis, basis, inverse, terms)


def scatter_sum(values, axes):
    count = lax.axis_size(axes)
    shares = lax.all_to_all(values, axes, 0, 0, tiled=True)
    return shares.reshape(count, values.shape[0] // count, values.shape[1]).sum(axis=0)


def gather(values, axes):
    count = lax.axis_size(axes)
    copies = jnp.broadcast_to(values[None], (count, *values.shape)).reshape(-1, values.shape[1])
    return lax.all_to_all(copies, axes, 0, 0, tiled=True)


def exchange_sum(values, axes):
    return gather(values, axes).reshape(lax.axis_size(axes), *values.shape).sum(axis=0)


def body(grads, errors, q_init):
    replicas = lax.axis_size(DP)
    power = power_terms(grads, errors, q_init)
    power = scatter_sum(power, "core")
    power = scatter_sum(power, ("y", "x"))
    power = exchange_sum(power, "near")
    power = exchange_sum(power, "far")
    power = gather(power, ("y", "x"))
    power = gather(power, "core")

    terms = factor_terms(grads, errors, power)
    terms = scatter_sum(terms, ("near", "y"))
    terms = exchange_sum(terms, "far")
    terms = gather(terms, ("near", "y"))

    basis, inverse = basis_of(power)
    own = lax.axis_index(DP).reshape(1)
    return outputs(grads, errors, basis, inverse, terms, replicas, own)


def solution(mesh):
    near = 4
    fine = Mesh(mesh.devices.reshape(4, near, 4, 4, 2), ("far", "near", "y", "x", "core"))
    placed = (P(DP, TENSOR), P(DP, TENSOR), P(TENSOR, None))
    return jax.shard_map(
        body,
        mesh=fine,
        in_specs=placed,
        out_specs=(P(DP, TENSOR), P(DP, TENSOR), P(TENSOR, None)),
        check_vma=False,
    )
```

time: 820 us -> 144 us (0.18)
  the two profiles are of different devices: /device:TPU:4 before, /device:TPU:8 now
where the time goes in v1:
time: 144 us; the launch traced here: 143 us
  blocking collectives  107 us (74%)
  Pallas kernels  22.8 us (16%)
  local copies, waits for them, and re-layouts  7.99 us (6%)
  starting transfers between devices  4.83 us (3%)
    all_to_all x5, blocking collectives, gather(): return lax.all_to_all(copies, axes, 0, 0, tiled=True)  69.5 us
    all_to_all x3, blocking collectives, scatter_sum(): shares = lax.all_to_all(values, axes, 0, 0, tiled=True)  37.1 us
    pallas_call x1, Pallas kernels, basis_of(): pl.pallas_call(basis_kernel, out_shape=(jax.ShapeDtypeStruct((rows, rank)...  14.9 us
    unnamed x18, local copies, waits for them, and re-layouts  7.16 us
    all_to_all x1, starting transfers between devices, gather(): return lax.all_to_all(copies, axes, 0, 0, tiled=True)  4.83 us
    pallas_call x1, Pallas kernels, outputs(): pl.pallas_call(functools.partial(output_kernel, replicas), grid_spec=pltp...  3.21 us
  transfers between devices with their start and end apart: 1, of which 0 were waited for; matrix products, arithmetic and copies ran while one was open for 0% of the time, Pallas kernels for 10%

profile of v1, /device:TPU:8, one launch (start us, length us, event | category | flops | bytes accessed | tf_op | source)
XLA Modules:
  0.0 143.2 jit_solution(16689563503441256987)
XLA Ops:
  0.6 0.0 copy-start
  0.6 1.4 copy-done
  2.0 0.0 copy-start.2
  2.0 1.4 copy-done.2
  3.4 0.0 copy-start.8
  3.5 0.9 copy-done.8
  4.4 2.6 %shard_map.58 = f32[2048,128]{1,0:T(8,128)S(1)} custom-call(bf16[2048,384]{1,0:T(8,128)(2,1)S(1)} %copy-done, bf16[2048,384]{1,0:T(8,128)(2,1)S(1)} %copy-done.2, f32[384,128]{1,0:T(8,128)S(1)} %copy-done.8), custom_call_target="tpu_custom_call" | custom-call | tf_op jit(solution)/shard_map/pallas_call | solution.py:53
  7.0 4.6 %all_to_all.67 = f32[2,1024,128]{2,1,0:T(8,128)S(1)} all-to-all(f32[2,1024,128]{2,1,0:T(8,128)S(1)} %bitcast.9), channel_id=1, replica_groups=mesh['far'=4,'near'=4,'y'=4,'x'=4,'core'=2] {'core'}, dimensions={0} | all-to-all | bytes 2097152 | tf_op jit(solution)/shard_map/all_to_all | solution.py:209
  11.6 0.1 reduce_sum.54
  11.7 17.9 %all_to_all.68 = f32[16,64,128]{2,1,0:T(8,128)S(1)} all-to-all(f32[16,64,128]{2,1,0:T(8,128)S(1)} %bitcast.13), channel_id=1, replica_groups=mesh['far'=4,'near'=4,'y'=4,'x'=4,'core'=2] {'y','x'}, dimensions={0} | all-to-all | bytes 1048576 | tf_op jit(solution)/shard_map/all_to_all | solution.py:209
  29.6 10.2 %all_to_all.69 = f32[4,64,128]{2,1,0:T(8,128)S(1)} all-to-all(f32[4,64,128]{2,1,0:T(8,128)S(1)} %broadcast_in_dim.14), channel_id=1, replica_groups=mesh['far'=4,'near'=4,'y'=4,'x'=4,'core'=2] {'near'}, dimensions={0} | all-to-all | bytes 262144 | tf_op jit(solution)/shard_map/all_to_all | solution.py:216
  39.8 25.6 %all_to_all.70 = f32[4,64,128]{2,1,0:T(8,128)S(1)} all-to-all(f32[4,64,128]{2,1,0:T(8,128)S(1)} %broadcast_in_dim.15), channel_id=1, replica_groups=mesh['far'=4,'near'=4,'y'=4,'x'=4,'core'=2] {'far'}, dimensions={0} | all-to-all | bytes 262144 | tf_op jit(solution)/shard_map/all_to_all | solution.py:216
  65.5 13.7 %all_to_all.71 = f32[16,64,128]{2,1,0:T(8,128)S(1)} all-to-all(f32[16,64,128]{2,1,0:T(8,128)S(1)} %broadcast_in_dim.16), channel_id=1, replica_groups=mesh['far'=4,'near'=4,'y'=4,'x'=4,'core'=2] {'y','x'}, dimensions={0} | all-to-all | bytes 1048576 | tf_op jit(solution)/shard_map/all_to_all | solution.py:216
  79.2 0.0 copy-start.3
  79.2 0.1 broadcast_in_dim.18
  79.2 4.8 %all_to_all.72 = f32[2,1024,128]{2,1,0:T(8,128)S(1)} all-to-all(f32[2,1024,128]{2,1,0:T(8,128)S(1)} %broadcast_in_dim.18), channel_id=1, replica_groups=mesh['far'=4,'near'=4,'y'=4,'x'=4,'core'=2] {'core'}, dimensions={0} | all-to-all | bytes 2097152 | tf_op jit(solution)/shard_map/all_to_all | solution.py:216
  84.1 0.0 copy-start.4
  84.1 0.0 copy-done.1
  84.1 0.0 copy-done.3
  84.1 2.1 %shard_map.60 = f32[128,384]{1,0:T(8,128)S(1)} custom-call(bf16[2048,384]{1,0:T(8,128)(2,1)S(1)} %copy-done.1, bf16[2048,384]{1,0:T(8,128)(2,1)S(1)} %copy-done.3, f32[2048,128]{1,0:T(8,128)S(1)} %bitcast.7), custom_call_target="tpu_custom_call" | custom-call | tf_op jit(solution)/shard_map/pallas_call | solution.py:147
  86.2 0.0 copy-done.4
  86.2 14.7 %all_to_all.73 = f32[16,8,384]{2,1,0:T(8,128)S(1)} all-to-all(f32[16,8,384]{2,1,0:T(8,128)S(1)} %bitcast.11), channel_id=1, replica_groups=mesh['far'=4,'near'=4,'y'=4,'x'=4,'core'=2] {'near','y'}, dimensions={0} | all-to-all | bytes 393216 | tf_op jit(solution)/shard_map/all_to_all | solution.py:209
  100.9 15.2 %all_to_all.74 = f32[4,8,384]{2,1,0:T(8,128)S(1)} all-to-all(f32[4,8,384]{2,1,0:T(8,128)S(1)} %broadcast_in_dim.19), channel_id=1, replica_groups=mesh['far'=4,'near'=4,'y'=4,'x'=4,'core'=2] {'far'}, dimensions={0} | all-to-all | bytes 98304 | tf_op jit(solution)/shard_map/all_to_all | solution.py:216
  116.2 0.7 broadcast_in_dim.20
  116.9 4.8 %all-to-all-start.8 = ((f32[16,8,384]{2,1,0:T(8,128)}), f32[16,8,384]{2,1,0:T(8,128)S(1)}, u32[]{:S(2)}, u32[]{:S(2)}) async-start(f32[16,8,384]{2,1,0:T(8,128)} %broadcast_in_dim.20), calls=%async_computation.8 | async-start | bytes 393216 | tf_op jit(solution)/shard_map/all_to_all | solution.py:216
  121.7 1.2 copy-done.5
  122.9 14.9 %shard_map.59 = (f32[2048,128]{1,0:T(8,128)S(1)}, f32[128,128]{1,0:T(8,128)S(1)}) custom-call(f32[2048,128]{1,0:T(8,128)S(1)} %bitcast.8), custom_call_target="tpu_custom_call" | custom-call | tf_op jit(solution)/shard_map/pallas_call | solution.py:116
  137.8 0.0 copy-start.6
  137.8 1.0 copy-done.6
  138.8 0.0 all-to-all-done.8
  138.8 1.2 copy-done.7
  140.0 3.2 %shard_map.61 = (bf16[32,384]{1,0:T(8,128)(2,1)}, bf16[2048,384]{1,0:T(8,128)(2,1)}, f32[384,128]{1,0:T(8,128)}) custom-call(s32[1]{0:T(128)} %bitcast.own_ref, bf16[2048,384]{1,0:T(8,128)(2,1)S(1)} %copy-done.1, bf16[2048,384]{1,0:T(8,128)(2,1)S(1)} %copy-done.3, f32[2048,128]{1,0:T(8,128)S(1)} %copy-done.7, f32[2048,128]{1,0:T(8,128)S(1)} %copy-done.7, ...), custom_call_target="tpu_custom_call" | custom-call | tf_op jit(solution)/shard_map/pallas_call | solution.py:182
  (12 shorter events, 0.2 us)
Async XLA Ops:
  0.6 1.4 copy-start
  2.0 1.4 copy-start.2
  3.4 0.9 copy-start.8
  79.2 4.9 %copy-start.1 = (bf16[2048,384]{1,0:T(8,128)(2,1)S(1)}, bf16[2048,384]{1,0:T(8,128)(2,1)}, u32[]{:S(2)}) copy-start(bf16[2048,384]{1,0:T(8,128)(2,1)} %grads_ref.5) | copy-start | bytes 4718596
  79.2 4.9 %copy-start.3 = (bf16[2048,384]{1,0:T(8,128)(2,1)S(1)}, bf16[2048,384]{1,0:T(8,128)(2,1)}, u32[]{:S(2)}) copy-start(bf16[2048,384]{1,0:T(8,128)(2,1)} %errors_ref.5) | copy-start | bytes 4718596
  84.1 2.1 %copy-start.4 = (f32[2,1024,128]{2,1,0:T(8,128)}, f32[2,1024,128]{2,1,0:T(8,128)S(1)}, u32[]{:S(2)}) copy-start(f32[2,1024,128]{2,1,0:T(8,128)S(1)} %all_to_all.72) | copy-start | bytes 3145732
  116.9 21.9 %all-to-all-start.8 = ((f32[16,8,384]{2,1,0:T(8,128)}), f32[16,8,384]{2,1,0:T(8,128)S(1)}, u32[]{:S(2)}, u32[]{:S(2)}) async-start(f32[16,8,384]{2,1,0:T(8,128)} %broadcast_in_dim.20), calls=%async_computation.8 | async-start | bytes 393216 | tf_op jit(solution)/shard_map/all_to_all | solution.py:216
  121.7 1.2 copy-start.5
  137.8 1.0 copy-start.6
  138.8 1.2 copy-start.7

commit v2 on v1

--- a/solution.py
+++ b/solution.py
@@ -14,7 +14,10 @@
 LANES_BY_LANES = (((1,), (1,)), ((), ()))
 WIDTH = 8
 TILE = 512
-VMEM_BYTES = 40 << 20
+VMEM_BYTES = 32 << 20
+POWER_VMEM_BYTES = 60 << 20
+OUTPUT_VMEM_BYTES = 52 << 20
+QR_COST = pl.CostEstimate(flops=7_000_000_000, bytes_accessed=1 << 20, transcendentals=0)
 
 DP = ("far", "near", "y")
 TENSOR = ("x", "core")
@@ -57,7 +60,7 @@
         in_specs=[tiled, tiled, whole((cols, rank))],
         out_specs=pl.BlockSpec((TILE, rank), lambda i: (i, 0)),
         scratch_shapes=[pltpu.VMEM((cols, 3 * rank), BF16)],
-        compiler_params=pltpu.CompilerParams(vmem_limit_bytes=VMEM_BYTES),
+        compiler_params=pltpu.CompilerParams(vmem_limit_bytes=POWER_VMEM_BYTES),
     )(grads, errors, q_init)
 
 
@@ -97,30 +100,51 @@
             work_ref[at : at + WIDTH, :] = jnp.where(inside, 0.0, rest) - terms[0]
 
 
-def basis_kernel(power_ref, basis_ref, inverse_ref, work_ref, step_ref):
-    first = None
-    source = power_ref
-    for _ in range(2):
-        gram = lax.dot_general(source[...], source[...], ROWS_BY_ROWS, precision=HIGHEST, preferred_element_type=F32)
-        inverse_factor(gram, work_ref, step_ref)
-        step = step_ref[...]
-        basis_ref[...] = lax.dot_general(source[...], step, LANES_BY_LANES, precision=HIGHEST, preferred_element_type=F32)
-        source = basis_ref
-        first = step if first is None else jnp.dot(step, first, precision=HIGHEST, preferred_element_type=F32)
-    inverse_ref[...] = first
-
-
-def basis_of(power):
-    rows, rank = power.shape
-    in_vmem = pl.BlockSpec(memory_space=pltpu.VMEM)
-    return pl.pallas_call(
-        basis_kernel,
-        out_shape=(jax.ShapeDtypeStruct((rows, rank), F32), jax.ShapeDtypeStruct((rank, rank), F32)),
-        in_specs=[in_vmem],
-        out_specs=(in_vmem, in_vmem),
-        scratch_shapes=[pltpu.VMEM((rank, rank), F32)] * 2,
+def first_pass_kernel(power_ref, first_ref, work_ref):
+    power = power_ref[...]
+    gram = lax.dot_general(power, power, ROWS_BY_ROWS, precision=HIGHEST, preferred_element_type=F32)
+    inverse_factor(gram, work_ref, first_ref)
+
+
+def second_pass_kernel(power_ref, first_ref, maps_ref, work_ref, second_ref):
+    rank = first_ref.shape[0]
+    first = lax.dot_general(
+        power_ref[...], first_ref[...], LANES_BY_LANES, precision=HIGHEST, preferred_element_type=F32
+    )
+    gram = lax.dot_general(first, first, ROWS_BY_ROWS, precision=HIGHEST, preferred_element_type=F32)
+    inverse_factor(gram, work_ref, second_ref)
+    both = jnp.dot(second_ref[...], first_ref[...], precision=HIGHEST, preferred_element_type=F32)
+    maps_ref[:rank, :] = both
+    maps_ref[rank:, :] = lax.dot_general(both, both, ROWS_BY_ROWS, precision=HIGHEST, preferred_element_type=F32)
+
+
+IN_VMEM = pl.BlockSpec(memory_space=pltpu.VMEM)
+
+
+def first_pass(power):
+    square = (power.shape[1],) * 2
+    return pl.pallas_call(
+        first_pass_kernel,
+        out_shape=jax.ShapeDtypeStruct(square, F32),
+        in_specs=[IN_VMEM],
+        out_specs=IN_VMEM,
+        scratch_shapes=[pltpu.VMEM(square, F32)],
         compiler_params=pltpu.CompilerParams(vmem_limit_bytes=VMEM_BYTES),
+        cost_estimate=QR_COST,
     )(power)
+
+
+def second_pass(power, first):
+    square = first.shape
+    return pl.pallas_call(
+        second_pass_kernel,
+        out_shape=jax.ShapeDtypeStruct((2 * square[0], square[1]), F32),
+        in_specs=[IN_VMEM, IN_VMEM],
+        out_specs=IN_VMEM,
+        scratch_shapes=[pltpu.VMEM(square, F32)] * 2,
+        compiler_params=pltpu.CompilerParams(vmem_limit_bytes=VMEM_BYTES),
+        cost_estimate=QR_COST,
+    )(power, first)
 
 
 def factor_kernel(grads_ref, errors_ref, power_ref, terms_ref, sum_ref):
@@ -155,7 +179,7 @@
     )(grads, errors, power)
 
 
-def output_kernel(replicas, own_ref, grads_ref, errors_ref, basis_ref, share_ref, inverse_ref, terms_ref,
+def output_kernel(replicas, own_ref, grads_ref, errors_ref, power_ref, share_ref, maps_ref, terms_ref,
                   avg_ref, new_ref, q_ref, split_ref):
     def decompressed(rows):
         high, low = pieces(rows, 2)
@@ -163,20 +187,21 @@
 
     @pl.when(pl.program_id(0) == 0)
     def _():
-        factor = jnp.dot(inverse_ref[...], terms_ref[...], precision=HIGHEST, preferred_element_type=F32)
-        factor = factor * (1.0 / replicas)
-        q_ref[...] = factor.T
-        high, low = pieces(factor, 2)
+        mapped = jnp.dot(maps_ref[...], terms_ref[...], precision=HIGHEST, preferred_element_type=F32)
+        mapped = mapped * (1.0 / replicas)
+        rank = power_ref.shape[1]
+        q_ref[...] = mapped[:rank, :].T
+        high, low = pieces(mapped[rank:, :], 2)
         split_ref[...] = jnp.concatenate([high, low, high], axis=0)
         avg_ref[...] = decompressed(share_ref[...]).astype(BF16)
 
     merged = grads_ref[...].astype(F32) + errors_ref[...].astype(F32)
-    new_ref[...] = (merged - decompressed(basis_ref[...])).astype(BF16)
-
-
-def outputs(grads, errors, basis, inverse, terms, replicas, own):
+    new_ref[...] = (merged - decompressed(power_ref[...])).astype(BF16)
+
+
+def outputs(grads, errors, power, maps, terms, replicas, own):
     rows, cols = grads.shape
-    rank = basis.shape[1]
+    rank = power.shape[1]
     share = rows // replicas
     tiled = pl.BlockSpec((TILE, cols), lambda i, own: (i, 0))
     return pl.pallas_call(
@@ -189,7 +214,7 @@
                 tiled,
                 pl.BlockSpec((TILE, rank), lambda i, own: (i, 0)),
                 pl.BlockSpec((share, rank), lambda i, own: (own[0], 0)),
-                whole((rank, rank)),
+                whole((2 * rank, rank)),
                 whole((rank, cols)),
             ],
             out_specs=(whole((share, cols)), tiled, whole((cols, rank))),
@@ -200,8 +225,8 @@
             jax.ShapeDtypeStruct((rows, cols), BF16),
             jax.ShapeDtypeStruct((cols, rank), F32),
         ),
-        compiler_params=pltpu.CompilerParams(vmem_limit_bytes=VMEM_BYTES),
-    )(own, grads, errors, basis, basis, inverse, terms)
+        compiler_params=pltpu.CompilerParams(vmem_limit_bytes=OUTPUT_VMEM_BYTES),
+    )(own, grads, errors, power, power, maps, terms)
 
 
 def scatter_sum(values, axes):
@@ -231,13 +256,15 @@
     power = gather(power, "core")
 
     terms = factor_terms(grads, errors, power)
+    first = first_pass(power)
     terms = scatter_sum(terms, ("near", "y"))
+    terms, first = lax.optimization_barrier((terms, first))
+    maps = second_pass(power, first)
     terms = exchange_sum(terms, "far")
+    terms, maps = lax.optimization_barrier((terms, maps))
     terms = gather(terms, ("near", "y"))
-
-    basis, inverse = basis_of(power)
     own = lax.axis_index(DP).reshape(1)
-    return outputs(grads, errors, basis, inverse, terms, replicas, own)
+    return outputs(grads, errors, power, maps, terms, replicas, own)
 
 
 def solution(mesh):

time: 144 us -> 138 us (0.958)
  blocking collectives: 107 us -> 77.8 us
  waiting for transfers between devices: 0.01 us -> 15.3 us
  starting transfers between devices: 4.83 us -> 14.6 us
  local copies, waits for them, and re-layouts: 7.99 us -> 1.46 us
  Pallas kernels: 22.8 us -> 27.2 us
    all_to_all x5 -> x4, blocking collectives: 69.5 us -> 54.3 us  [gather(): return lax.all_to_all(copies, axes, 0, 0, tiled=True)]
    all_to_all x3 -> x2, blocking collectives: 37.1 us -> 23.6 us  [scatter_sum(): shares = lax.all_to_all(values, axes, 0, 0, tiled=True)]
    all_to_all x1 -> x2, waiting for transfers between devices: 0.01 us -> 12.2 us  [gather(): return lax.all_to_all(copies, axes, 0, 0, tiled=True)]
    unnamed x18 -> x4, local copies, waits for them, and re-layouts: 7.16 us -> 0.01 us
    all_to_all x0 -> x1, starting transfers between devices: none -> 6.34 us  [scatter_sum(): shares = lax.all_to_all(values, axes, 0, 0, tiled=True)]
    all_to_all x1 -> x2, starting transfers between devices: 4.83 us -> 8.29 us  [gather(): return lax.all_to_all(copies, axes, 0, 0, tiled=True)]
    all_to_all x0 -> x1, waiting for transfers between devices: none -> 3.04 us  [scatter_sum(): shares = lax.all_to_all(values, axes, 0, 0, tiled=True)]
    pallas_call x1, Pallas kernels: 2.62 us -> 5.15 us  [power_terms(): pl.pallas_call(power_kernel, grid=(rows // TILE,), out_shape=jax.ShapeDty...]
  transfers between devices with their start and end apart: 1 -> 3, of which waited for: 0 -> 3; matrix products, arithmetic and copies ran while one was open for 0% -> 0% of each run, Pallas kernels for 10% -> 10%
where the time goes in v2:
time: 138 us; the launch traced here: 137 us
  blocking collectives  77.8 us (56%)
  Pallas kernels  27.2 us (20%)
  waiting for transfers between devices  15.3 us (11%)
  starting transfers between devices  14.6 us (11%)
  local copies, waits for them, and re-layouts  1.46 us (1%)
    all_to_all x4, blocking collectives, gather(): return lax.all_to_all(copies, axes, 0, 0, tiled=True)  54.3 us
    all_to_all x2, blocking collectives, scatter_sum(): shares = lax.all_to_all(values, axes, 0, 0, tiled=True)  23.6 us
    all_to_all x2, waiting for transfers between devices, gather(): return lax.all_to_all(copies, axes, 0, 0, tiled=True)  12.2 us
    pallas_call x1, Pallas kernels, second_pass(): pl.pallas_call(second_pass_kernel, out_shape=jax.ShapeDtypeStruct((2 * sq...  8.56 us
    all_to_all x2, starting transfers between devices, gather(): return lax.all_to_all(copies, axes, 0, 0, tiled=True)  8.29 us
    all_to_all x1, starting transfers between devices, scatter_sum(): shares = lax.all_to_all(values, axes, 0, 0, tiled=True)  6.34 us
    pallas_call x1, Pallas kernels, first_pass(): pl.pallas_call(first_pass_kernel, out_shape=jax.ShapeDtypeStruct(square,...  5.52 us
    pallas_call x1, Pallas kernels, outputs(): pl.pallas_call(functools.partial(output_kernel, replicas), grid_spec=pltp...  5.27 us
  transfers between devices with their start and end apart: 3, of which 3 were waited for; matrix products, arithmetic and copies ran while one was open for 0% of the time, Pallas kernels for 10%

profile of v2, /device:TPU:8, one launch (start us, length us, event | category | flops | bytes accessed | tf_op | source)
XLA Modules:
  0.0 137.3 jit_solution(5662309229669363122)
XLA Ops:
  0.6 5.1 %shard_map.58 = f32[2048,128]{1,0:T(8,128)} custom-call(bf16[2048,384]{1,0:T(8,128)(2,1)} %grads_ref.5, bf16[2048,384]{1,0:T(8,128)(2,1)} %errors_ref.5, f32[384,128]{1,0:T(8,128)} %q_ref.1), custom_call_target="tpu_custom_call" | custom-call | tf_op jit(solution)/shard_map/pallas_call | solution.py:56
  5.8 5.7 %all_to_all.67 = f32[2,1024,128]{2,1,0:T(8,128)S(1)} all-to-all(f32[2,1024,128]{2,1,0:T(8,128)} %bitcast.13), channel_id=1, replica_groups=mesh['far'=4,'near'=4,'y'=4,'x'=4,'core'=2] {'core'}, dimensions={0} | all-to-all | bytes 2097152 | tf_op jit(solution)/shard_map/all_to_all | solution.py:234
  11.5 0.1 reduce_sum.54
  11.6 17.9 %all_to_all.68 = f32[16,64,128]{2,1,0:T(8,128)S(1)} all-to-all(f32[16,64,128]{2,1,0:T(8,128)S(1)} %bitcast.15), channel_id=1, replica_groups=mesh['far'=4,'near'=4,'y'=4,'x'=4,'core'=2] {'y','x'}, dimensions={0} | all-to-all | bytes 1048576 | tf_op jit(solution)/shard_map/all_to_all | solution.py:234
  29.5 10.2 %all_to_all.69 = f32[4,64,128]{2,1,0:T(8,128)S(1)} all-to-all(f32[4,64,128]{2,1,0:T(8,128)S(1)} %broadcast_in_dim.14), channel_id=1, replica_groups=mesh['far'=4,'near'=4,'y'=4,'x'=4,'core'=2] {'near'}, dimensions={0} | all-to-all | bytes 262144 | tf_op jit(solution)/shard_map/all_to_all | solution.py:241
  39.7 25.6 %all_to_all.70 = f32[4,64,128]{2,1,0:T(8,128)S(1)} all-to-all(f32[4,64,128]{2,1,0:T(8,128)S(1)} %broadcast_in_dim.15), channel_id=1, replica_groups=mesh['far'=4,'near'=4,'y'=4,'x'=4,'core'=2] {'far'}, dimensions={0} | all-to-all | bytes 262144 | tf_op jit(solution)/shard_map/all_to_all | solution.py:241
  65.4 13.7 %all_to_all.71 = f32[16,64,128]{2,1,0:T(8,128)S(1)} all-to-all(f32[16,64,128]{2,1,0:T(8,128)S(1)} %broadcast_in_dim.16), channel_id=1, replica_groups=mesh['far'=4,'near'=4,'y'=4,'x'=4,'core'=2] {'y','x'}, dimensions={0} | all-to-all | bytes 1048576 | tf_op jit(solution)/shard_map/all_to_all | solution.py:241
  79.0 0.0 copy-start
  79.0 0.0 copy-start.1
  79.0 0.1 broadcast_in_dim.18
  79.1 4.8 %all_to_all.72 = f32[2,1024,128]{2,1,0:T(8,128)S(1)} all-to-all(f32[2,1024,128]{2,1,0:T(8,128)S(1)} %broadcast_in_dim.18), channel_id=1, replica_groups=mesh['far'=4,'near'=4,'y'=4,'x'=4,'core'=2] {'core'}, dimensions={0} | all-to-all | bytes 2097152 | tf_op jit(solution)/shard_map/all_to_all | solution.py:241
  84.0 0.0 copy-done
  84.0 0.0 copy-done.1
  84.0 2.8 %shard_map.59 = f32[128,384]{1,0:T(8,128)} custom-call(bf16[2048,384]{1,0:T(8,128)(2,1)S(1)} %copy-done, bf16[2048,384]{1,0:T(8,128)(2,1)S(1)} %copy-done.1, f32[2048,128]{1,0:T(8,128)S(1)} %bitcast.7), custom_call_target="tpu_custom_call" | custom-call | tf_op jit(solution)/shard_map/pallas_call | solution.py:171
  86.7 6.3 %all-to-all-start.6 = ((f32[16,8,384]{2,1,0:T(8,128)}), f32[16,8,384]{2,1,0:T(8,128)S(1)}, u32[]{:S(2)}, u32[]{:S(2)}) async-start(f32[16,8,384]{2,1,0:T(8,128)} %bitcast.5), calls=%async_computation.6 | async-start | bytes 393216 | tf_op jit(solution)/shard_map/all_to_all | solution.py:234
  93.1 5.5 %shard_map.60.first_ref = f32[128,128]{1,0:T(8,128)S(1)} custom-call(f32[2048,128]{1,0:T(8,128)S(1)} %bitcast.8), custom_call_target="tpu_custom_call" | custom-call | flops 7000000000 | bytes 1048576 | tf_op jit(solution)/shard_map/pallas_call | solution.py:126
  98.6 3.0 %all-to-all-done.6 = f32[16,8,384]{2,1,0:T(8,128)S(1)} async-done(((f32[16,8,384]{2,1,0:T(8,128)}), f32[16,8,384]{2,1,0:T(8,128)S(1)}, u32[]{:S(2)}, u32[]{:S(2)}) %all-to-all-start.6) | async-done | bytes 196640 | tf_op jit(solution)/shard_map/all_to_all | solution.py:234
  101.6 0.6 broadcast_in_dim.19
  102.3 3.5 %all-to-all-start.7 = ((f32[4,8,384]{2,1,0:T(8,128)}), f32[4,8,384]{2,1,0:T(8,128)S(1)}, u32[]{:S(2)}, u32[]{:S(2)}) async-start(f32[4,8,384]{2,1,0:T(8,128)} %broadcast_in_dim.19), calls=%async_computation.7 | async-start | bytes 98304 | tf_op jit(solution)/shard_map/all_to_all | solution.py:241
  105.7 8.6 %shard_map.61.maps_ref = f32[256,128]{1,0:T(8,128)S(1)} custom-call(f32[2048,128]{1,0:T(8,128)S(1)} %bitcast.9, f32[128,128]{1,0:T(8,128)S(1)} %shard_map.60.first_ref), custom_call_target="tpu_custom_call" | custom-call | flops 7000000000 | bytes 1048576 | tf_op jit(solution)/shard_map/pallas_call | solution.py:139
  114.3 4.1 %all-to-all-done.7 = f32[4,8,384]{2,1,0:T(8,128)S(1)} async-done(((f32[4,8,384]{2,1,0:T(8,128)}), f32[4,8,384]{2,1,0:T(8,128)S(1)}, u32[]{:S(2)}, u32[]{:S(2)}) %all-to-all-start.7) | async-done | bytes 49184 | tf_op jit(solution)/shard_map/all_to_all | solution.py:241
  118.4 0.7 broadcast_in_dim.20
  119.1 4.8 %all-to-all-start.8 = ((f32[16,8,384]{2,1,0:T(8,128)}), f32[16,8,384]{2,1,0:T(8,128)S(1)}, u32[]{:S(2)}, u32[]{:S(2)}) async-start(f32[16,8,384]{2,1,0:T(8,128)} %broadcast_in_dim.20), calls=%async_computation.8 | async-start | bytes 393216 | tf_op jit(solution)/shard_map/all_to_all | solution.py:241
  123.9 8.1 %all-to-all-done.8 = f32[16,8,384]{2,1,0:T(8,128)S(1)} async-done(((f32[16,8,384]{2,1,0:T(8,128)}), f32[16,8,384]{2,1,0:T(8,128)S(1)}, u32[]{:S(2)}, u32[]{:S(2)}) %all-to-all-start.8) | async-done | bytes 196640 | tf_op jit(solution)/shard_map/all_to_all | solution.py:241
  132.0 5.3 %shard_map.62 = (bf16[32,384]{1,0:T(8,128)(2,1)}, bf16[2048,384]{1,0:T(8,128)(2,1)}, f32[384,128]{1,0:T(8,128)}) custom-call(s32[1]{0:T(128)} %bitcast.own_ref, bf16[2048,384]{1,0:T(8,128)(2,1)} %grads_ref.5, bf16[2048,384]{1,0:T(8,128)(2,1)} %errors_ref.5, f32[2048,128]{1,0:T(8,128)S(1)} %bitcast.10, f32[2048,128]{1,0:T(8,128)S(1)} %bitcast.11, ...), custom_call_target="tpu_custom_call" | custom-call | tf_op jit(solution)/shard_map/pallas_call | solution.py:207
  (8 shorter events, 0.1 us)
Async XLA Ops:
  79.0 4.9 %copy-start = (bf16[2048,384]{1,0:T(8,128)(2,1)S(1)}, bf16[2048,384]{1,0:T(8,128)(2,1)}, u32[]{:S(2)}) copy-start(bf16[2048,384]{1,0:T(8,128)(2,1)} %grads_ref.5) | copy-start | bytes 4718596
  79.0 4.9 %copy-start.1 = (bf16[2048,384]{1,0:T(8,128)(2,1)S(1)}, bf16[2048,384]{1,0:T(8,128)(2,1)}, u32[]{:S(2)}) copy-start(bf16[2048,384]{1,0:T(8,128)(2,1)} %errors_ref.5) | copy-start | bytes 4718596
  86.7 14.9 %all-to-all-start.6 = ((f32[16,8,384]{2,1,0:T(8,128)}), f32[16,8,384]{2,1,0:T(8,128)S(1)}, u32[]{:S(2)}, u32[]{:S(2)}) async-start(f32[16,8,384]{2,1,0:T(8,128)} %bitcast.5), calls=%async_computation.6 | async-start | bytes 393216 | tf_op jit(solution)/shard_map/all_to_all | solution.py:234
  102.3 16.1 %all-to-all-start.7 = ((f32[4,8,384]{2,1,0:T(8,128)}), f32[4,8,384]{2,1,0:T(8,128)S(1)}, u32[]{:S(2)}, u32[]{:S(2)}) async-start(f32[4,8,384]{2,1,0:T(8,128)} %broadcast_in_dim.19), calls=%async_computation.7 | async-start | bytes 98304 | tf_op jit(solution)/shard_map/all_to_all | solution.py:241
  119.1 13.0 %all-to-all-start.8 = ((f32[16,8,384]{2,1,0:T(8,128)}), f32[16,8,384]{2,1,0:T(8,128)S(1)}, u32[]{:S(2)}, u32[]{:S(2)}) async-start(f32[16,8,384]{2,1,0:T(8,128)} %broadcast_in_dim.20), calls=%async_computation.8 | async-start | bytes 393216 | tf_op jit(solution)/shard_map/all_to_all | solution.py:241

commit v3 on v2

--- a/solution.py
+++ b/solution.py
@@ -14,13 +14,13 @@
 LANES_BY_LANES = (((1,), (1,)), ((), ()))
 WIDTH = 8
 TILE = 512
-VMEM_BYTES = 32 << 20
-POWER_VMEM_BYTES = 60 << 20
-OUTPUT_VMEM_BYTES = 52 << 20
+CHUNK = 256
+VMEM_BYTES = 16 << 20
 QR_COST = pl.CostEstimate(flops=7_000_000_000, bytes_accessed=1 << 20, transcendentals=0)
 
 DP = ("far", "near", "y")
 TENSOR = ("x", "core")
+PLANE = ("y", "x", "core")
 
 
 def pieces(values, count):
@@ -36,32 +36,67 @@
     return pl.BlockSpec(ref_shape, lambda *_: (0,) * len(ref_shape))
 
 
-def power_kernel(grads_ref, errors_ref, q_ref, power_ref, split_ref):
-    rank = q_ref.shape[1]
-
-    @pl.when(pl.program_id(0) == 0)
-    def _():
-        for k, part in enumerate(pieces(q_ref[...], 3)):
-            split_ref[:, k * rank : (k + 1) * rank] = part
-
-    products = jnp.dot(grads_ref[...], split_ref[...], preferred_element_type=F32)
-    products += jnp.dot(errors_ref[...], split_ref[...], preferred_element_type=F32)
-    power_ref[...] = products[:, :rank] + (products[:, rank : 2 * rank] + products[:, 2 * rank :])
+def load(sources, buffers, sems):
+    chunks = sources[0].shape[0] // CHUNK
+
+    def copy(k, n):
+        rows = pl.ds(k * CHUNK, CHUNK)
+        return pltpu.make_async_copy(sources[n].at[rows], buffers[n].at[rows], sems.at[k, n])
+
+    for k in range(chunks):
+        for n in range(len(sources)):
+            copy(k, n).start()
+
+    def wait(k):
+        for n in range(len(sources)):
+            copy(k, n).wait()
+
+    return wait
+
+
+def power_kernel(grads_ref, errors_ref, q_ref, power_ref, held_g, held_e, held_q, split_ref, q_sem, sems):
+    cols, rank = q_ref.shape
+    q_copy = pltpu.make_async_copy(q_ref, held_q, q_sem)
+    q_copy.start()
+    wait = load((grads_ref, errors_ref), (held_g, held_e), sems)
+    q_copy.wait()
+    for k, part in enumerate(pieces(held_q[...], 3)):
+        split_ref[:cols, k * rank : (k + 1) * rank] = part
+        split_ref[cols:, k * rank : (k + 1) * rank] = part
+    for k in range(grads_ref.shape[0] // CHUNK):
+        wait(k)
+        rows = slice(k * CHUNK, (k + 1) * CHUNK)
+        both = jnp.concatenate([held_g[rows, :], held_e[rows, :]], axis=1)
+        products = jnp.dot(both, split_ref[...], preferred_element_type=F32)
+        power_ref[rows, :] = products[:, :rank] + (products[:, rank : 2 * rank] + products[:, 2 * rank :])
+
+
+IN_VMEM = pl.BlockSpec(memory_space=pltpu.VMEM)
+IN_HBM = pl.BlockSpec(memory_space=pltpu.HBM)
+
+
+def in_hbm(values):
+    return pltpu.with_memory_space_constraint(values, pltpu.HBM)
 
 
 def power_terms(grads, errors, q_init):
     rows, cols = grads.shape
     rank = q_init.shape[1]
-    tiled = pl.BlockSpec((TILE, cols), lambda i: (i, 0))
     return pl.pallas_call(
         power_kernel,
-        grid=(rows // TILE,),
         out_shape=jax.ShapeDtypeStruct((rows, rank), F32),
-        in_specs=[tiled, tiled, whole((cols, rank))],
-        out_specs=pl.BlockSpec((TILE, rank), lambda i: (i, 0)),
-        scratch_shapes=[pltpu.VMEM((cols, 3 * rank), BF16)],
-        compiler_params=pltpu.CompilerParams(vmem_limit_bytes=POWER_VMEM_BYTES),
-    )(grads, errors, q_init)
+        in_specs=[IN_HBM] * 3,
+        out_specs=IN_VMEM,
+        scratch_shapes=[
+            pltpu.VMEM((rows, cols), BF16),
+            pltpu.VMEM((rows, cols), BF16),
+            pltpu.VMEM((cols, rank), F32),
+            pltpu.VMEM((2 * cols, 3 * rank), BF16),
+            pltpu.SemaphoreType.DMA,
+            pltpu.SemaphoreType.DMA((rows // CHUNK, 2)),
+        ],
+        compiler_params=pltpu.CompilerParams(vmem_limit_bytes=52 << 20),
+    )(in_hbm(grads), in_hbm(errors), in_hbm(q_init))
 
 
 def inverse_factor(gram, work_ref, inverse_ref):
@@ -118,9 +153,6 @@
     maps_ref[rank:, :] = lax.dot_general(both, both, ROWS_BY_ROWS, precision=HIGHEST, preferred_element_type=F32)
 
 
-IN_VMEM = pl.BlockSpec(memory_space=pltpu.VMEM)
-
-
 def first_pass(power):
     square = (power.shape[1],) * 2
     return pl.pallas_call(
@@ -129,7 +161,7 @@
         in_specs=[IN_VMEM],
         out_specs=IN_VMEM,
         scratch_shapes=[pltpu.VMEM(square, F32)],
-        compiler_params=pltpu.CompilerParams(vmem_limit_bytes=VMEM_BYTES),
+        compiler_params=pltpu.CompilerParams(vmem_limit_bytes=32 << 20),
         cost_estimate=QR_COST,
     )(power)
 
@@ -142,16 +174,18 @@
         in_specs=[IN_VMEM, IN_VMEM],
         out_specs=IN_VMEM,
         scratch_shapes=[pltpu.VMEM(square, F32)] * 2,
-        compiler_params=pltpu.CompilerParams(vmem_limit_bytes=VMEM_BYTES),
+        compiler_params=pltpu.CompilerParams(vmem_limit_bytes=32 << 20),
         cost_estimate=QR_COST,
     )(power, first)
 
 
 def factor_kernel(grads_ref, errors_ref, power_ref, terms_ref, sum_ref):
     rank = power_ref.shape[1]
+    cols = grads_ref.shape[1]
     split = jnp.concatenate(pieces(power_ref[...], 2), axis=1)
-    products = lax.dot_general(split, grads_ref[...], ROWS_BY_ROWS, preferred_element_type=F32)
-    products += lax.dot_general(split, errors_ref[...], ROWS_BY_ROWS, preferred_element_type=F32)
+    both = jnp.concatenate([grads_ref[...], errors_ref[...]], axis=1)
+    products = lax.dot_general(split, both, ROWS_BY_ROWS, preferred_element_type=F32)
+    products = products[:, :cols] + products[:, cols:]
 
     @pl.when(pl.program_id(0) == 0)
     def _():
@@ -175,58 +209,63 @@
         in_specs=[tiled, tiled, pl.BlockSpec((TILE, rank), lambda i: (i, 0))],
         out_specs=whole((rank, cols)),
         scratch_shapes=[pltpu.VMEM((2 * rank, cols), F32)],
-        compiler_params=pltpu.CompilerParams(vmem_limit_bytes=VMEM_BYTES),
+        compiler_params=pltpu.CompilerParams(vmem_limit_bytes=32 << 20),
     )(grads, errors, power)
 
 
-def output_kernel(replicas, own_ref, grads_ref, errors_ref, power_ref, share_ref, maps_ref, terms_ref,
-                  avg_ref, new_ref, q_ref, split_ref):
+def output_kernel(replicas, own_ref, grads_ref, errors_ref, power_ref, maps_ref, terms_ref, avg_ref, new_ref, q_ref,
+                  held_g, held_e, held_new, split_ref, sems, out_sems):
+    rank = power_ref.shape[1]
+    share = avg_ref.shape[0]
+    wait = load((grads_ref, errors_ref), (held_g, held_e), sems)
+
     def decompressed(rows):
         high, low = pieces(rows, 2)
         return jnp.dot(jnp.concatenate([high, high, low], axis=1), split_ref[...], preferred_element_type=F32)
 
-    @pl.when(pl.program_id(0) == 0)
-    def _():
-        mapped = jnp.dot(maps_ref[...], terms_ref[...], precision=HIGHEST, preferred_element_type=F32)
-        mapped = mapped * (1.0 / replicas)
-        rank = power_ref.shape[1]
-        q_ref[...] = mapped[:rank, :].T
-        high, low = pieces(mapped[rank:, :], 2)
-        split_ref[...] = jnp.concatenate([high, low, high], axis=0)
-        avg_ref[...] = decompressed(share_ref[...]).astype(BF16)
-
-    merged = grads_ref[...].astype(F32) + errors_ref[...].astype(F32)
-    new_ref[...] = (merged - decompressed(power_ref[...])).astype(BF16)
+    mapped = jnp.dot(maps_ref[...], terms_ref[...], precision=HIGHEST, preferred_element_type=F32)
+    mapped = mapped * (1.0 / replicas)
+    high, low = pieces(mapped[rank:, :], 2)
+    split_ref[...] = jnp.concatenate([high, low, high], axis=0)
+    writes = []
+    for k in range(grads_ref.shape[0] // CHUNK):
+        wait(k)
+        rows = slice(k * CHUNK, (k + 1) * CHUNK)
+        merged = held_g[rows, :].astype(F32) + held_e[rows, :].astype(F32)
+        held_new[rows, :] = (merged - decompressed(power_ref[rows, :])).astype(BF16)
+        chunk = pl.ds(k * CHUNK, CHUNK)
+        writes.append(pltpu.make_async_copy(held_new.at[chunk], new_ref.at[chunk], out_sems.at[k]))
+        writes[-1].start()
+    own = power_ref[pl.ds(pl.multiple_of(own_ref[0] * share, share), share), :]
+    avg_ref[...] = decompressed(own).astype(BF16)
+    q_ref[...] = mapped[:rank, :].T
+    for write in writes:
+        write.wait()
 
 
 def outputs(grads, errors, power, maps, terms, replicas, own):
     rows, cols = grads.shape
     rank = power.shape[1]
-    share = rows // replicas
-    tiled = pl.BlockSpec((TILE, cols), lambda i, own: (i, 0))
+    chunks = rows // CHUNK
     return pl.pallas_call(
         functools.partial(output_kernel, replicas),
-        grid_spec=pltpu.PrefetchScalarGridSpec(
-            num_scalar_prefetch=1,
-            grid=(rows // TILE,),
-            in_specs=[
-                tiled,
-                tiled,
-                pl.BlockSpec((TILE, rank), lambda i, own: (i, 0)),
-                pl.BlockSpec((share, rank), lambda i, own: (own[0], 0)),
-                whole((2 * rank, rank)),
-                whole((rank, cols)),
-            ],
-            out_specs=(whole((share, cols)), tiled, whole((cols, rank))),
-            scratch_shapes=[pltpu.VMEM((3 * rank, cols), BF16)],
-        ),
+        in_specs=[pl.BlockSpec(memory_space=pltpu.SMEM), IN_HBM, IN_HBM, IN_VMEM, IN_VMEM, IN_VMEM],
+        out_specs=(IN_VMEM, IN_HBM, IN_VMEM),
         out_shape=(
-            jax.ShapeDtypeStruct((share, cols), BF16),
+            jax.ShapeDtypeStruct((rows // replicas, cols), BF16),
             jax.ShapeDtypeStruct((rows, cols), BF16),
             jax.ShapeDtypeStruct((cols, rank), F32),
         ),
-        compiler_params=pltpu.CompilerParams(vmem_limit_bytes=OUTPUT_VMEM_BYTES),
-    )(own, grads, errors, power, power, maps, terms)
+        scratch_shapes=[
+            pltpu.VMEM((rows, cols), BF16),
+            pltpu.VMEM((rows, cols), BF16),
+            pltpu.VMEM((rows, cols), BF16),
+            pltpu.VMEM((3 * rank, cols), BF16),
+            pltpu.SemaphoreType.DMA((chunks, 2)),
+            pltpu.SemaphoreType.DMA((chunks,)),
+        ],
+        compiler_params=pltpu.CompilerParams(vmem_limit_bytes=52 << 20),
+    )(own, in_hbm(grads), in_hbm(errors), power, maps, terms)
 
 
 def scatter_sum(values, axes):
@@ -248,12 +287,10 @@
 def body(grads, errors, q_init):
     replicas = lax.axis_size(DP)
     power = power_terms(grads, errors, q_init)
-    power = scatter_sum(power, "core")
-    power = scatter_sum(power, ("y", "x"))
+    power = scatter_sum(power, PLANE)
     power = exchange_sum(power, "near")
     power = exchange_sum(power, "far")
-    power = gather(power, ("y", "x"))
-    power = gather(power, "core")
+    power = gather(power, PLANE)
 
     terms = factor_terms(grads, errors, power)
     first = first_pass(power)
@@ -261,9 +298,9 @@
     terms, first = lax.optimization_barrier((terms, first))
     maps = second_pass(power, first)
     terms = exchange_sum(terms, "far")
-    terms, maps = lax.optimization_barrier((terms, maps))
+    own = lax.axis_index(DP).reshape(1)
+    terms, maps, own = lax.optimization_barrier((terms, maps, own))
     terms = gather(terms, ("near", "y"))
-    own = lax.axis_index(DP).reshape(1)
     return outputs(grads, errors, power, maps, terms, replicas, own)
 
 

time: 138 us -> 142 us (1.029)
  the two profiles are of different devices: /device:TPU:8 before, /device:TPU:2 now
where the time goes in v3:
time: 142 us
  blocking collectives  96.5 us (68%)
  Pallas kernels  26.9 us (19%)
  waiting for transfers between devices  8.07 us (6%)
  starting transfers between devices  7.47 us (5%)
  local copies, waits for them, and re-layouts  2.01 us (1%)
    all_to_all x4, blocking collectives, gather(): return lax.all_to_all(copies, axes, 0, 0, tiled=True)  71.7 us
    all_to_all x1, blocking collectives, scatter_sum(): shares = lax.all_to_all(values, axes, 0, 0, tiled=True)  24.8 us
    pallas_call x1, Pallas kernels, second_pass(): pl.pallas_call(second_pass_kernel, out_shape=jax.ShapeDtypeStruct((2 * sq...  8.56 us
    pallas_call x1, Pallas kernels, first_pass(): pl.pallas_call(first_pass_kernel, out_shape=jax.ShapeDtypeStruct(square,...  5.52 us
    pallas_call x1, Pallas kernels, power_terms(): pl.pallas_call(power_kernel, out_shape=jax.ShapeDtypeStruct((rows, rank),...  5.14 us
    pallas_call x1, Pallas kernels, outputs(): pl.pallas_call(functools.partial(output_kernel, replicas), in_specs=[pl.B...  5.09 us
    all_to_all x1, waiting for transfers between devices, gather(): return lax.all_to_all(copies, axes, 0, 0, tiled=True)  4.09 us
    all_to_all x1, starting transfers between devices, scatter_sum(): shares = lax.all_to_all(values, axes, 0, 0, tiled=True)  4.02 us
  transfers between devices with their start and end apart: 2, of which 2 were waited for; matrix products, arithmetic and copies ran while one was open for 0% of the time, Pallas kernels for 10%

profile of v3, /device:TPU:2, one launch (start us, length us, event | category | flops | bytes accessed | tf_op | source)
XLA Modules:
  0.0 142.0 jit_solution(6824834651920032352)
XLA Ops:
  0.6 5.1 %shard_map.58 = f32[2048,128]{1,0:T(8,128)S(1)} custom-call(bf16[2048,384]{1,0:T(8,128)(2,1)} %grads_ref.5, bf16[2048,384]{1,0:T(8,128)(2,1)} %errors_ref.5, f32[384,128]{1,0:T(8,128)} %q_ref.1), custom_call_target="tpu_custom_call" | custom-call | tf_op jit(solution)/shard_map/pallas_call | solution.py:85
  5.8 24.8 %all_to_all.52 = f32[32,64,128]{2,1,0:T(8,128)S(1)} all-to-all(f32[32,64,128]{2,1,0:T(8,128)S(1)} %bitcast.9), channel_id=1, replica_groups=mesh['far'=4,'near'=4,'y'=4,'x'=4,'core'=2] {'y','x','core'}, dimensions={0} | all-to-all | bytes 2097152 | tf_op jit(solution)/shard_map/all_to_all | solution.py:273
  30.6 0.1 reduce_sum.45
  30.7 10.7 %all_to_all.53 = f32[4,64,128]{2,1,0:T(8,128)S(1)} all-to-all(f32[4,64,128]{2,1,0:T(8,128)S(1)} %broadcast_in_dim.10), channel_id=1, replica_groups=mesh['far'=4,'near'=4,'y'=4,'x'=4,'core'=2] {'near'}, dimensions={0} | all-to-all | bytes 262144 | tf_op jit(solution)/shard_map/all_to_all | solution.py:280
  41.4 26.6 %all_to_all.54 = f32[4,64,128]{2,1,0:T(8,128)S(1)} all-to-all(f32[4,64,128]{2,1,0:T(8,128)S(1)} %broadcast_in_dim.11), channel_id=1, replica_groups=mesh['far'=4,'near'=4,'y'=4,'x'=4,'core'=2] {'far'}, dimensions={0} | all-to-all | bytes 262144 | tf_op jit(solution)/shard_map/all_to_all | solution.py:280
  68.0 0.0 copy-start
  68.0 0.0 copy-start.1
  68.0 0.1 broadcast_in_dim.12
  68.1 21.6 %all_to_all.55 = f32[32,64,128]{2,1,0:T(8,128)S(1)} all-to-all(f32[32,64,128]{2,1,0:T(8,128)S(1)} %broadcast_in_dim.12), channel_id=1, replica_groups=mesh['far'=4,'near'=4,'y'=4,'x'=4,'core'=2] {'y','x','core'}, dimensions={0} | all-to-all | bytes 2097152 | tf_op jit(solution)/shard_map/all_to_all | solution.py:280
  89.7 0.0 copy-start.2
  89.7 0.0 copy-done
  89.7 0.0 copy-done.1
  89.7 2.6 %shard_map.59 = f32[128,384]{1,0:T(8,128)} custom-call(bf16[2048,384]{1,0:T(8,128)(2,1)S(1)} %copy-done, bf16[2048,384]{1,0:T(8,128)(2,1)S(1)} %copy-done.1, f32[2048,128]{1,0:T(8,128)S(1)} %bitcast.5), custom_call_target="tpu_custom_call" | custom-call | tf_op jit(solution)/shard_map/pallas_call | solution.py:205
  92.3 0.0 copy-done.2
  92.3 4.0 %all-to-all-start.4 = ((f32[16,8,384]{2,1,0:T(8,128)}), f32[16,8,384]{2,1,0:T(8,128)S(1)}, u32[]{:S(2)}, u32[]{:S(2)}) async-start(f32[16,8,384]{2,1,0:T(8,128)} %bitcast.2), calls=%async_computation.4 | async-start | bytes 393216 | tf_op jit(solution)/shard_map/all_to_all | solution.py:273
  96.3 0.0 copy-start.3
  96.3 1.2 copy-done.3
  97.6 0.0 copy-start.4
  97.6 5.5 %shard_map.60.first_ref = f32[128,128]{1,0:T(8,128)S(1)} custom-call(f32[2048,128]{1,0:T(8,128)S(1)} %bitcast.6), custom_call_target="tpu_custom_call" | custom-call | flops 7000000000 | bytes 1048576 | tf_op jit(solution)/shard_map/pallas_call | solution.py:158
  103.1 4.0 %all-to-all-done.4 = f32[16,8,384]{2,1,0:T(8,128)S(1)} async-done(((f32[16,8,384]{2,1,0:T(8,128)}), f32[16,8,384]{2,1,0:T(8,128)S(1)}, u32[]{:S(2)}, u32[]{:S(2)}) %all-to-all-start.4) | async-done | bytes 196640 | tf_op jit(solution)/shard_map/all_to_all | solution.py:273
  107.1 0.6 broadcast_in_dim.13
  107.7 3.5 %all-to-all-start.5 = ((f32[4,8,384]{2,1,0:T(8,128)}), f32[4,8,384]{2,1,0:T(8,128)S(1)}, u32[]{:S(2)}, u32[]{:S(2)}) async-start(f32[4,8,384]{2,1,0:T(8,128)} %broadcast_in_dim.13), calls=%async_computation.5 | async-start | bytes 98304 | tf_op jit(solution)/shard_map/all_to_all | solution.py:280
  111.2 0.0 copy-done.4
  111.2 8.6 %shard_map.61.maps_ref = f32[256,128]{1,0:T(8,128)S(1)} custom-call(f32[2048,128]{1,0:T(8,128)S(1)} %bitcast.7, f32[128,128]{1,0:T(8,128)S(1)} %shard_map.60.first_ref), custom_call_target="tpu_custom_call" | custom-call | flops 7000000000 | bytes 1048576 | tf_op jit(solution)/shard_map/pallas_call | solution.py:171
  119.8 4.1 %all-to-all-done.5 = f32[4,8,384]{2,1,0:T(8,128)S(1)} async-done(((f32[4,8,384]{2,1,0:T(8,128)}), f32[4,8,384]{2,1,0:T(8,128)S(1)}, u32[]{:S(2)}, u32[]{:S(2)}) %all-to-all-start.5) | async-done | bytes 49184 | tf_op jit(solution)/shard_map/all_to_all | solution.py:280
  123.9 12.9 %all_to_all.56 = f32[16,8,384]{2,1,0:T(8,128)S(1)} all-to-all(f32[16,8,384]{2,1,0:T(8,128)S(1)} %broadcast_in_dim.14), channel_id=1, replica_groups=mesh['far'=4,'near'=4,'y'=4,'x'=4,'core'=2] {'near','y'}, dimensions={0} | all-to-all | bytes 393216 | tf_op jit(solution)/shard_map/all_to_all | solution.py:280
  136.7 5.1 %shard_map.62 = (bf16[32,384]{1,0:T(8,128)(2,1)}, bf16[2048,384]{1,0:T(8,128)(2,1)}, f32[384,128]{1,0:T(8,128)}) custom-call(s32[1]{0:T(128)} %bitcast.3.own_ref, bf16[2048,384]{1,0:T(8,128)(2,1)} %grads_ref.5, bf16[2048,384]{1,0:T(8,128)(2,1)} %errors_ref.5, f32[2048,128]{1,0:T(8,128)S(1)} %bitcast.8, f32[256,128]{1,0:T(8,128)S(1)} %shard_map.61.maps_ref, ...), custom_call_target="tpu_custom_call" | custom-call | tf_op jit(solution)/shard_map/pallas_call | solution.py:250
  (7 shorter events, 0.1 us)
Async XLA Ops:
  68.0 21.8 %copy-start = (bf16[2048,384]{1,0:T(8,128)(2,1)S(1)}, bf16[2048,384]{1,0:T(8,128)(2,1)}, u32[]{:S(2)}) copy-start(bf16[2048,384]{1,0:T(8,128)(2,1)} %grads_ref.5) | copy-start | bytes 4718596
  68.0 21.7 %copy-start.1 = (bf16[2048,384]{1,0:T(8,128)(2,1)S(1)}, bf16[2048,384]{1,0:T(8,128)(2,1)}, u32[]{:S(2)}) copy-start(bf16[2048,384]{1,0:T(8,128)(2,1)} %errors_ref.5) | copy-start | bytes 4718596
  89.7 2.6 %copy-start.2 = (f32[32,64,128]{2,1,0:T(8,128)}, f32[32,64,128]{2,1,0:T(8,128)S(1)}, u32[]{:S(2)}) copy-start(f32[32,64,128]{2,1,0:T(8,128)S(1)} %all_to_all.55) | copy-start | bytes 3145732
  92.3 14.8 %all-to-all-start.4 = ((f32[16,8,384]{2,1,0:T(8,128)}), f32[16,8,384]{2,1,0:T(8,128)S(1)}, u32[]{:S(2)}, u32[]{:S(2)}) async-start(f32[16,8,384]{2,1,0:T(8,128)} %bitcast.2), calls=%async_computation.4 | async-start | bytes 393216 | tf_op jit(solution)/shard_map/all_to_all | solution.py:273
  96.3 1.2 copy-start.3
  97.6 13.6 %copy-start.4 = (f32[32,64,128]{2,1,0:T(8,128)S(1)}, f32[32,64,128]{2,1,0:T(8,128)}, u32[]{:S(2)}) copy-start(f32[32,64,128]{2,1,0:T(8,128)} %copy-done.2) | copy-start | bytes 3145732
  107.7 16.1 %all-to-all-start.5 = ((f32[4,8,384]{2,1,0:T(8,128)}), f32[4,8,384]{2,1,0:T(8,128)S(1)}, u32[]{:S(2)}, u32[]{:S(2)}) async-start(f32[4,8,384]{2,1,0:T(8,128)} %broadcast_in_dim.13), calls=%async_computation.5 | async-start | bytes 98304 | tf_op jit(solution)/shard_map/all_to_all | solution.py:280

commit v4 on v3

--- a/solution.py
+++ b/solution.py
@@ -13,14 +13,12 @@
 ROWS_BY_ROWS = (((0,), (0,)), ((), ()))
 LANES_BY_LANES = (((1,), (1,)), ((), ()))
 WIDTH = 8
-TILE = 512
-CHUNK = 256
+CHUNK = 1024
 VMEM_BYTES = 16 << 20
 QR_COST = pl.CostEstimate(flops=7_000_000_000, bytes_accessed=1 << 20, transcendentals=0)
 
 DP = ("far", "near", "y")
 TENSOR = ("x", "core")
-PLANE = ("y", "x", "core")
 
 
 def pieces(values, count):
@@ -30,10 +28,6 @@
         parts.append(part)
         values = values - part.astype(F32)
     return parts
-
-
-def whole(ref_shape):
-    return pl.BlockSpec(ref_shape, lambda *_: (0,) * len(ref_shape))
 
 
 def load(sources, buffers, sems):
@@ -179,80 +173,77 @@
     )(power, first)
 
 
-def factor_kernel(grads_ref, errors_ref, power_ref, terms_ref, sum_ref):
-    rank = power_ref.shape[1]
-    cols = grads_ref.shape[1]
+def factor_kernel(grads_ref, errors_ref, power_ref, terms_ref):
+    rank, cols = terms_ref.shape
     split = jnp.concatenate(pieces(power_ref[...], 2), axis=1)
     both = jnp.concatenate([grads_ref[...], errors_ref[...]], axis=1)
     products = lax.dot_general(split, both, ROWS_BY_ROWS, preferred_element_type=F32)
     products = products[:, :cols] + products[:, cols:]
-
-    @pl.when(pl.program_id(0) == 0)
-    def _():
-        sum_ref[...] = products
-
-    @pl.when(pl.program_id(0) > 0)
-    def _():
-        sum_ref[...] += products
-
-    terms_ref[...] = sum_ref[:rank, :] + sum_ref[rank:, :]
+    terms_ref[...] = products[:rank, :] + products[rank:, :]
 
 
 def factor_terms(grads, errors, power):
-    rows, cols = grads.shape
-    rank = power.shape[1]
-    tiled = pl.BlockSpec((TILE, cols), lambda i: (i, 0))
     return pl.pallas_call(
         factor_kernel,
-        grid=(rows // TILE,),
-        out_shape=jax.ShapeDtypeStruct((rank, cols), F32),
-        in_specs=[tiled, tiled, pl.BlockSpec((TILE, rank), lambda i: (i, 0))],
-        out_specs=whole((rank, cols)),
-        scratch_shapes=[pltpu.VMEM((2 * rank, cols), F32)],
+        out_shape=jax.ShapeDtypeStruct((power.shape[1], grads.shape[1]), F32),
+        in_specs=[IN_VMEM] * 3,
+        out_specs=IN_VMEM,
         compiler_params=pltpu.CompilerParams(vmem_limit_bytes=32 << 20),
     )(grads, errors, power)
 
 
 def output_kernel(replicas, own_ref, grads_ref, errors_ref, power_ref, maps_ref, terms_ref, avg_ref, new_ref, q_ref,
-                  held_g, held_e, held_new, split_ref, sems, out_sems):
+                  held_g, held_e, held_new, held_avg, held_q, sems, out_sems, avg_sem, q_sem):
     rank = power_ref.shape[1]
     share = avg_ref.shape[0]
     wait = load((grads_ref, errors_ref), (held_g, held_e), sems)
-
-    def decompressed(rows):
-        high, low = pieces(rows, 2)
-        return jnp.dot(jnp.concatenate([high, high, low], axis=1), split_ref[...], preferred_element_type=F32)
-
-    mapped = jnp.dot(maps_ref[...], terms_ref[...], precision=HIGHEST, preferred_element_type=F32)
-    mapped = mapped * (1.0 / replicas)
-    high, low = pieces(mapped[rank:, :], 2)
-    split_ref[...] = jnp.concatenate([high, low, high], axis=0)
     writes = []
+
+    def write(held, out, sem):
+        writes.append(pltpu.make_async_copy(held, out, sem))
+        writes[-1].start()
+
+    def left(values):
+        high, low = pieces(values, 2)
+        return jnp.concatenate([high, high, low], axis=1)
+
+    def right(values):
+        high, low = pieces(values, 2)
+        return jnp.concatenate([high, low, high], axis=0)
+
+    def product(values, stacked):
+        return jnp.dot(left(values), stacked, preferred_element_type=F32)
+
+    terms = right(terms_ref[...] * (1.0 / replicas))
+    mapped = right(product(maps_ref[rank:, :], terms))
     for k in range(grads_ref.shape[0] // CHUNK):
         wait(k)
         rows = slice(k * CHUNK, (k + 1) * CHUNK)
         merged = held_g[rows, :].astype(F32) + held_e[rows, :].astype(F32)
-        held_new[rows, :] = (merged - decompressed(power_ref[rows, :])).astype(BF16)
+        held_new[rows, :] = (merged - product(power_ref[rows, :], mapped)).astype(BF16)
         chunk = pl.ds(k * CHUNK, CHUNK)
-        writes.append(pltpu.make_async_copy(held_new.at[chunk], new_ref.at[chunk], out_sems.at[k]))
-        writes[-1].start()
-    own = power_ref[pl.ds(pl.multiple_of(own_ref[0] * share, share), share), :]
-    avg_ref[...] = decompressed(own).astype(BF16)
-    q_ref[...] = mapped[:rank, :].T
-    for write in writes:
-        write.wait()
+        write(held_new.at[chunk], new_ref.at[chunk], out_sems.at[k])
+        if k == 0:
+            own = power_ref[pl.ds(pl.multiple_of(own_ref[0] * share, share), share), :]
+            held_avg[...] = product(own, mapped).astype(BF16)
+            write(held_avg, avg_ref, avg_sem)
+            held_q[...] = product(maps_ref[:rank, :], terms).T
+            write(held_q, q_ref, q_sem)
+    for copy in writes:
+        copy.wait()
 
 
 def outputs(grads, errors, power, maps, terms, replicas, own):
     rows, cols = grads.shape
     rank = power.shape[1]
+    share = rows // replicas
     chunks = rows // CHUNK
     return pl.pallas_call(
         functools.partial(output_kernel, replicas),
         in_specs=[pl.BlockSpec(memory_space=pltpu.SMEM), IN_HBM, IN_HBM, IN_VMEM, IN_VMEM, IN_VMEM],
-        out_specs=(IN_VMEM, IN_HBM, IN_VMEM),
+        out_specs=(IN_HBM, IN_HBM, IN_HBM),
         out_shape=(
-            jax.ShapeDtypeStruct((rows // replicas, cols), BF16),
+            jax.ShapeDtypeStruct((share, cols), BF16),
             jax.ShapeDtypeStruct((rows, cols), BF16),
             jax.ShapeDtypeStruct((cols, rank), F32),
         ),
@@ -260,9 +251,12 @@
             pltpu.VMEM((rows, cols), BF16),
             pltpu.VMEM((rows, cols), BF16),
             pltpu.VMEM((rows, cols), BF16),
-            pltpu.VMEM((3 * rank, cols), BF16),
+            pltpu.VMEM((share, cols), BF16),
+            pltpu.VMEM((cols, rank), F32),
             pltpu.SemaphoreType.DMA((chunks, 2)),
             pltpu.SemaphoreType.DMA((chunks,)),
+            pltpu.SemaphoreType.DMA,
+            pltpu.SemaphoreType.DMA,
         ],
         compiler_params=pltpu.CompilerParams(vmem_limit_bytes=52 << 20),
     )(own, in_hbm(grads), in_hbm(errors), power, maps, terms)
@@ -287,19 +281,21 @@
 def body(grads, errors, q_init):
     replicas = lax.axis_size(DP)
     power = power_terms(grads, errors, q_init)
-    power = scatter_sum(power, PLANE)
+    power = scatter_sum(power, "core")
+    power = scatter_sum(power, ("y", "x"))
     power = exchange_sum(power, "near")
     power = exchange_sum(power, "far")
-    power = gather(power, PLANE)
+    power = gather(power, ("y", "x"))
+    power = gather(power, "core")
 
     terms = factor_terms(grads, errors, power)
     first = first_pass(power)
+    own = lax.axis_index(DP).reshape(1)
     terms = scatter_sum(terms, ("near", "y"))
+    terms, first, own = lax.optimization_barrier((terms, first, own))
+    terms = exchange_sum(terms, "far")
     terms, first = lax.optimization_barrier((terms, first))
     maps = second_pass(power, first)
-    terms = exchange_sum(terms, "far")
-    own = lax.axis_index(DP).reshape(1)
-    terms, maps, own = lax.optimization_barrier((terms, maps, own))
     terms = gather(terms, ("near", "y"))
     return outputs(grads, errors, power, maps, terms, replicas, own)
 

time: 142 us -> 133 us (0.937)
  the two profiles are of different devices: /device:TPU:2 before, /device:TPU:8 now
where the time goes in v4:
time: 133 us
  blocking collectives  92.4 us (69%)
  Pallas kernels  23.3 us (18%)
  starting transfers between devices  11.8 us (9%)
  local copies, waits for them, and re-layouts  2.07 us (2%)
  waiting for transfers between devices  1.81 us (1%)
    all_to_all x5, blocking collectives, gather(): return lax.all_to_all(copies, axes, 0, 0, tiled=True)  70 us
    all_to_all x2, blocking collectives, scatter_sum(): shares = lax.all_to_all(values, axes, 0, 0, tiled=True)  22.5 us
    pallas_call x1, Pallas kernels, second_pass(): pl.pallas_call(second_pass_kernel, out_shape=jax.ShapeDtypeStruct((2 * sq...  8.56 us
    all_to_all x1, starting transfers between devices, scatter_sum(): shares = lax.all_to_all(values, axes, 0, 0, tiled=True)  6.33 us
    pallas_call x1, Pallas kernels, first_pass(): pl.pallas_call(first_pass_kernel, out_shape=jax.ShapeDtypeStruct(square,...  5.52 us
    all_to_all x1, starting transfers between devices, gather(): return lax.all_to_all(copies, axes, 0, 0, tiled=True)  5.45 us
    pallas_call x1, Pallas kernels, outputs(): pl.pallas_call(functools.partial(output_kernel, replicas), in_specs=[pl.B...  3.83 us
    pallas_call x1, Pallas kernels, power_terms(): pl.pallas_call(power_kernel, out_shape=jax.ShapeDtypeStruct((rows, rank),...  3.72 us
  transfers between devices with their start and end apart: 2, of which 1 were waited for; matrix products, arithmetic and copies ran while one was open for 0% of the time, Pallas kernels for 11%

profile of v4, /device:TPU:8, one launch (start us, length us, event | category | flops | bytes accessed | tf_op | source)
XLA Modules:
  0.0 132.5 jit_solution(10151917621131188273)
XLA Ops:
  0.6 3.7 %shard_map.58 = f32[2048,128]{1,0:T(8,128)S(1)} custom-call(bf16[2048,384]{1,0:T(8,128)(2,1)} %grads_ref.5, bf16[2048,384]{1,0:T(8,128)(2,1)} %errors_ref.5, f32[384,128]{1,0:T(8,128)} %q_ref.1), custom_call_target="tpu_custom_call" | custom-call | tf_op jit(solution)/shard_map/pallas_call | solution.py:79
  4.4 4.6 %all_to_all.67 = f32[2,1024,128]{2,1,0:T(8,128)S(1)} all-to-all(f32[2,1024,128]{2,1,0:T(8,128)S(1)} %bitcast.11), channel_id=1, replica_groups=mesh['far'=4,'near'=4,'y'=4,'x'=4,'core'=2] {'core'}, dimensions={0} | all-to-all | bytes 2097152 | tf_op jit(solution)/shard_map/all_to_all | solution.py:267
  8.9 0.1 reduce_sum.54
  9.0 17.9 %all_to_all.68 = f32[16,64,128]{2,1,0:T(8,128)S(1)} all-to-all(f32[16,64,128]{2,1,0:T(8,128)S(1)} %bitcast.14), channel_id=1, replica_groups=mesh['far'=4,'near'=4,'y'=4,'x'=4,'core'=2] {'y','x'}, dimensions={0} | all-to-all | bytes 1048576 | tf_op jit(solution)/shard_map/all_to_all | solution.py:267
  27.0 10.2 %all_to_all.69 = f32[4,64,128]{2,1,0:T(8,128)S(1)} all-to-all(f32[4,64,128]{2,1,0:T(8,128)S(1)} %broadcast_in_dim.14), channel_id=1, replica_groups=mesh['far'=4,'near'=4,'y'=4,'x'=4,'core'=2] {'near'}, dimensions={0} | all-to-all | bytes 262144 | tf_op jit(solution)/shard_map/all_to_all | solution.py:274
  37.2 25.6 %all_to_all.70 = f32[4,64,128]{2,1,0:T(8,128)S(1)} all-to-all(f32[4,64,128]{2,1,0:T(8,128)S(1)} %broadcast_in_dim.15), channel_id=1, replica_groups=mesh['far'=4,'near'=4,'y'=4,'x'=4,'core'=2] {'far'}, dimensions={0} | all-to-all | bytes 262144 | tf_op jit(solution)/shard_map/all_to_all | solution.py:274
  62.8 13.7 %all_to_all.71 = f32[16,64,128]{2,1,0:T(8,128)S(1)} all-to-all(f32[16,64,128]{2,1,0:T(8,128)S(1)} %broadcast_in_dim.16), channel_id=1, replica_groups=mesh['far'=4,'near'=4,'y'=4,'x'=4,'core'=2] {'y','x'}, dimensions={0} | all-to-all | bytes 1048576 | tf_op jit(solution)/shard_map/all_to_all | solution.py:274
  76.5 0.0 copy-start
  76.5 0.0 copy-start.1
  76.5 0.1 broadcast_in_dim.18
  76.6 4.8 %all_to_all.72 = f32[2,1024,128]{2,1,0:T(8,128)S(1)} all-to-all(f32[2,1024,128]{2,1,0:T(8,128)S(1)} %broadcast_in_dim.18), channel_id=1, replica_groups=mesh['far'=4,'near'=4,'y'=4,'x'=4,'core'=2] {'core'}, dimensions={0} | all-to-all | bytes 2097152 | tf_op jit(solution)/shard_map/all_to_all | solution.py:274
  81.4 0.0 copy-start.2
  81.4 0.0 copy-done
  81.4 0.0 copy-done.1
  81.4 1.7 %shard_map.59 = f32[128,384]{1,0:T(8,128)} custom-call(bf16[2048,384]{1,0:T(8,128)(2,1)S(1)} %copy-done, bf16[2048,384]{1,0:T(8,128)(2,1)S(1)} %copy-done.1, f32[2048,128]{1,0:T(8,128)S(1)} %bitcast.7), custom_call_target="tpu_custom_call" | custom-call | tf_op jit(solution)/shard_map/pallas_call | solution.py:186
  83.2 0.0 copy-done.2
  83.2 6.3 %all-to-all-start.6 = ((f32[16,8,384]{2,1,0:T(8,128)}), f32[16,8,384]{2,1,0:T(8,128)S(1)}, u32[]{:S(2)}, u32[]{:S(2)}) async-start(f32[16,8,384]{2,1,0:T(8,128)} %bitcast.4), calls=%async_computation.6 | async-start | bytes 393216 | tf_op jit(solution)/shard_map/all_to_all | solution.py:267
  89.5 0.0 copy-start.3
  89.5 1.2 copy-done.3
  90.7 0.0 copy-start.4
  90.7 5.5 %shard_map.60.first_ref = f32[128,128]{1,0:T(8,128)S(1)} custom-call(f32[2048,128]{1,0:T(8,128)S(1)} %bitcast.8), custom_call_target="tpu_custom_call" | custom-call | flops 7000000000 | bytes 1048576 | tf_op jit(solution)/shard_map/pallas_call | solution.py:152
  96.2 1.8 %all-to-all-done.6 = f32[16,8,384]{2,1,0:T(8,128)S(1)} async-done(((f32[16,8,384]{2,1,0:T(8,128)}), f32[16,8,384]{2,1,0:T(8,128)S(1)}, u32[]{:S(2)}, u32[]{:S(2)}) %all-to-all-start.6) | async-done | bytes 196640 | tf_op jit(solution)/shard_map/all_to_all | solution.py:267
  98.1 15.7 %all_to_all.73 = f32[4,8,384]{2,1,0:T(8,128)S(1)} all-to-all(f32[4,8,384]{2,1,0:T(8,128)S(1)} %broadcast_in_dim.19), channel_id=1, replica_groups=mesh['far'=4,'near'=4,'y'=4,'x'=4,'core'=2] {'far'}, dimensions={0} | all-to-all | bytes 98304 | tf_op jit(solution)/shard_map/all_to_all | solution.py:274
  113.8 0.7 broadcast_in_dim.20
  114.5 5.5 %all-to-all-start.8 = ((f32[16,8,384]{2,1,0:T(8,128)}), f32[16,8,384]{2,1,0:T(8,128)S(1)}, u32[]{:S(2)}, u32[]{:S(2)}) async-start(f32[16,8,384]{2,1,0:T(8,128)} %broadcast_in_dim.20), calls=%async_computation.8 | async-start | bytes 393216 | tf_op jit(solution)/shard_map/all_to_all | solution.py:274
  119.9 0.0 copy-done.4
  119.9 8.6 %shard_map.61.maps_ref = f32[256,128]{1,0:T(8,128)S(1)} custom-call(f32[2048,128]{1,0:T(8,128)S(1)} %bitcast.9, f32[128,128]{1,0:T(8,128)S(1)} %shard_map.60.first_ref), custom_call_target="tpu_custom_call" | custom-call | flops 7000000000 | bytes 1048576 | tf_op jit(solution)/shard_map/pallas_call | solution.py:165
  128.5 0.0 all-to-all-done.8
  128.5 3.8 %shard_map.62 = (bf16[32,384]{1,0:T(8,128)(2,1)}, bf16[2048,384]{1,0:T(8,128)(2,1)}, f32[384,128]{1,0:T(8,128)}) custom-call(s32[1]{0:T(128)} %bitcast.5.own_ref, bf16[2048,384]{1,0:T(8,128)(2,1)} %grads_ref.5, bf16[2048,384]{1,0:T(8,128)(2,1)} %errors_ref.5, f32[2048,128]{1,0:T(8,128)S(1)} %bitcast.10, f32[256,128]{1,0:T(8,128)S(1)} %shard_map.61.maps_ref, ...), custom_call_target="tpu_custom_call" | custom-call | tf_op jit(solution)/shard_map/pallas_call | solution.py:241
  (9 shorter events, 0.2 us)
Async XLA Ops:
  76.5 4.9 %copy-start = (bf16[2048,384]{1,0:T(8,128)(2,1)S(1)}, bf16[2048,384]{1,0:T(8,128)(2,1)}, u32[]{:S(2)}) copy-start(bf16[2048,384]{1,0:T(8,128)(2,1)} %grads_ref.5) | copy-start | bytes 4718596
  76.5 4.9 %copy-start.1 = (bf16[2048,384]{1,0:T(8,128)(2,1)S(1)}, bf16[2048,384]{1,0:T(8,128)(2,1)}, u32[]{:S(2)}) copy-start(bf16[2048,384]{1,0:T(8,128)(2,1)} %errors_ref.5) | copy-start | bytes 4718596
  81.4 1.7 %copy-start.2 = (f32[2,1024,128]{2,1,0:T(8,128)}, f32[2,1024,128]{2,1,0:T(8,128)S(1)}, u32[]{:S(2)}) copy-start(f32[2,1024,128]{2,1,0:T(8,128)S(1)} %all_to_all.72) | copy-start | bytes 3145732
  83.2 14.9 %all-to-all-start.6 = ((f32[16,8,384]{2,1,0:T(8,128)}), f32[16,8,384]{2,1,0:T(8,128)S(1)}, u32[]{:S(2)}, u32[]{:S(2)}) async-start(f32[16,8,384]{2,1,0:T(8,128)} %bitcast.4), calls=%async_computation.6 | async-start | bytes 393216 | tf_op jit(solution)/shard_map/all_to_all | solution.py:267
  89.5 1.2 copy-start.3
  90.7 29.2 %copy-start.4 = (f32[2,1024,128]{2,1,0:T(8,128)S(1)}, f32[2,1024,128]{2,1,0:T(8,128)}, u32[]{:S(2)}) copy-start(f32[2,1024,128]{2,1,0:T(8,128)} %copy-done.2) | copy-start | bytes 3145732
  114.5 14.0 %all-to-all-start.8 = ((f32[16,8,384]{2,1,0:T(8,128)}), f32[16,8,384]{2,1,0:T(8,128)S(1)}, u32[]{:S(2)}, u32[]{:S(2)}) async-start(f32[16,8,384]{2,1,0:T(8,128)} %broadcast_in_dim.20), calls=%async_computation.8 | async-start | bytes 393216 | tf_op jit(solution)/shard_map/all_to_all | solution.py:274

commit v5 on v4

--- a/solution.py
+++ b/solution.py
@@ -17,7 +17,9 @@
 VMEM_BYTES = 16 << 20
 QR_COST = pl.CostEstimate(flops=7_000_000_000, bytes_accessed=1 << 20, transcendentals=0)
 
-DP = ("far", "near", "y")
+NEAR = 4
+
+DP = ("z", "y")
 TENSOR = ("x", "core")
 
 
@@ -129,19 +131,17 @@
             work_ref[at : at + WIDTH, :] = jnp.where(inside, 0.0, rest) - terms[0]
 
 
-def first_pass_kernel(power_ref, first_ref, work_ref):
+def first_pass_kernel(power_ref, first_ref, gram_ref, work_ref):
     power = power_ref[...]
     gram = lax.dot_general(power, power, ROWS_BY_ROWS, precision=HIGHEST, preferred_element_type=F32)
     inverse_factor(gram, work_ref, first_ref)
-
-
-def second_pass_kernel(power_ref, first_ref, maps_ref, work_ref, second_ref):
+    first = lax.dot_general(power, first_ref[...], LANES_BY_LANES, precision=HIGHEST, preferred_element_type=F32)
+    gram_ref[...] = lax.dot_general(first, first, ROWS_BY_ROWS, precision=HIGHEST, preferred_element_type=F32)
+
+
+def second_pass_kernel(first_ref, gram_ref, maps_ref, work_ref, second_ref):
     rank = first_ref.shape[0]
-    first = lax.dot_general(
-        power_ref[...], first_ref[...], LANES_BY_LANES, precision=HIGHEST, preferred_element_type=F32
-    )
-    gram = lax.dot_general(first, first, ROWS_BY_ROWS, precision=HIGHEST, preferred_element_type=F32)
-    inverse_factor(gram, work_ref, second_ref)
+    inverse_factor(gram_ref[...], work_ref, second_ref)
     both = jnp.dot(second_ref[...], first_ref[...], precision=HIGHEST, preferred_element_type=F32)
     maps_ref[:rank, :] = both
     maps_ref[rank:, :] = lax.dot_general(both, both, ROWS_BY_ROWS, precision=HIGHEST, preferred_element_type=F32)
@@ -151,26 +151,26 @@
     square = (power.shape[1],) * 2
     return pl.pallas_call(
         first_pass_kernel,
-        out_shape=jax.ShapeDtypeStruct(square, F32),
+        out_shape=(jax.ShapeDtypeStruct(square, F32),) * 2,
         in_specs=[IN_VMEM],
-        out_specs=IN_VMEM,
+        out_specs=(IN_VMEM, IN_VMEM),
         scratch_shapes=[pltpu.VMEM(square, F32)],
-        compiler_params=pltpu.CompilerParams(vmem_limit_bytes=32 << 20),
+        compiler_params=pltpu.CompilerParams(vmem_limit_bytes=VMEM_BYTES),
         cost_estimate=QR_COST,
     )(power)
 
 
-def second_pass(power, first):
-    square = first.shape
+def second_pass(first, gram):
+    rank = gram.shape[0]
     return pl.pallas_call(
         second_pass_kernel,
-        out_shape=jax.ShapeDtypeStruct((2 * square[0], square[1]), F32),
+        out_shape=jax.ShapeDtypeStruct((2 * rank, rank), F32),
         in_specs=[IN_VMEM, IN_VMEM],
         out_specs=IN_VMEM,
-        scratch_shapes=[pltpu.VMEM(square, F32)] * 2,
-        compiler_params=pltpu.CompilerParams(vmem_limit_bytes=32 << 20),
+        scratch_shapes=[pltpu.VMEM((rank, rank), F32)] * 2,
+        compiler_params=pltpu.CompilerParams(vmem_limit_bytes=VMEM_BYTES),
         cost_estimate=QR_COST,
-    )(power, first)
+    )(first, gram)
 
 
 def factor_kernel(grads_ref, errors_ref, power_ref, terms_ref):
@@ -262,47 +262,68 @@
     )(own, in_hbm(grads), in_hbm(errors), power, maps, terms)
 
 
-def scatter_sum(values, axes):
-    count = lax.axis_size(axes)
-    shares = lax.all_to_all(values, axes, 0, 0, tiled=True)
+def exchange(values, axes, groups):
+    return lax.all_to_all(values, axes, 0, 0, axis_index_groups=groups, tiled=True)
+
+
+def members(axes, groups):
+    return lax.axis_size(axes) if groups is None else len(groups[0])
+
+
+def scatter_sum(values, axes, groups=None):
+    count = members(axes, groups)
+    shares = exchange(values, axes, groups)
     return shares.reshape(count, values.shape[0] // count, values.shape[1]).sum(axis=0)
 
 
-def gather(values, axes):
-    count = lax.axis_size(axes)
-    copies = jnp.broadcast_to(values[None], (count, *values.shape)).reshape(-1, values.shape[1])
-    return lax.all_to_all(copies, axes, 0, 0, tiled=True)
-
-
-def exchange_sum(values, axes):
-    return gather(values, axes).reshape(lax.axis_size(axes), *values.shape).sum(axis=0)
+def gather(values, axes, groups=None):
+    copies = jnp.broadcast_to(values[None], (members(axes, groups), *values.shape)).reshape(-1, values.shape[1])
+    return exchange(copies, axes, groups)
+
+
+def exchange_sum(values, axes, groups):
+    return gather(values, axes, groups).reshape(members(axes, groups), *values.shape).sum(axis=0)
+
+
+def z_groups(length, width):
+    blocks = length // NEAR
+
+    def device(block, share, y):
+        turn = NEAR // 2 if 2 * block >= blocks else 0
+        return (block * NEAR + (share + turn) % NEAR) * width + y
+
+    shares = [(share, y) for share in range(NEAR) for y in range(width)]
+    near = [[device(block, *share) for share in shares] for block in range(blocks)]
+    far = [[device(block, *share) for block in range(blocks)] for share in shares]
+    return near, far
 
 
 def body(grads, errors, q_init):
     replicas = lax.axis_size(DP)
     power = power_terms(grads, errors, q_init)
+    near, far = z_groups(lax.axis_size("z"), 1)
     power = scatter_sum(power, "core")
     power = scatter_sum(power, ("y", "x"))
-    power = exchange_sum(power, "near")
-    power = exchange_sum(power, "far")
+    power = exchange_sum(power, "z", near)
+    power = exchange_sum(power, "z", far)
     power = gather(power, ("y", "x"))
     power = gather(power, "core")
 
+    near, far = z_groups(lax.axis_size("z"), lax.axis_size("y"))
     terms = factor_terms(grads, errors, power)
     first = first_pass(power)
     own = lax.axis_index(DP).reshape(1)
-    terms = scatter_sum(terms, ("near", "y"))
+    terms = scatter_sum(terms, DP, near)
     terms, first, own = lax.optimization_barrier((terms, first, own))
-    terms = exchange_sum(terms, "far")
+    terms = exchange_sum(terms, DP, far)
     terms, first = lax.optimization_barrier((terms, first))
-    maps = second_pass(power, first)
-    terms = gather(terms, ("near", "y"))
+    maps = second_pass(*first)
+    terms = gather(terms, DP, near)
     return outputs(grads, errors, power, maps, terms, replicas, own)
 
 
 def solution(mesh):
-    near = 4
-    fine = Mesh(mesh.devices.reshape(4, near, 4, 4, 2), ("far", "near", "y", "x", "core"))
+    fine = Mesh(mesh.devices.reshape(16, 4, 4, 2), ("z", "y", "x", "core"))
     placed = (P(DP, TENSOR), P(DP, TENSOR), P(TENSOR, None))
     return jax.shard_map(
         body,

time: 133 us -> 132 us (level)
  the two profiles are of different devices: /device:TPU:8 before, /device:TPU:2 now
where the time goes in v5:
time: 132 us
  blocking collectives  89.2 us (68%)
  Pallas kernels  23.6 us (18%)
  starting transfers between devices  11.5 us (9%)
  waiting for transfers between devices  4.2 us (3%)
  local copies, waits for them, and re-layouts  2.07 us (2%)
    all_to_all x7, blocking collectives, exchange(): lax.all_to_all(values, axes, 0, 0, axis_index_groups=groups, tiled=True)  89.2 us
    all_to_all x2, starting transfers between devices, exchange(): lax.all_to_all(values, axes, 0, 0, axis_index_groups=groups, tiled=True)  11.5 us
    pallas_call x1, Pallas kernels, first_pass(): pl.pallas_call(first_pass_kernel, out_shape=(jax.ShapeDtypeStruct(square,...  9.12 us
    pallas_call x1, Pallas kernels, second_pass(): pl.pallas_call(second_pass_kernel, out_shape=jax.ShapeDtypeStruct((2 * ra...  5.23 us
    all_to_all x2, waiting for transfers between devices, exchange(): lax.all_to_all(values, axes, 0, 0, axis_index_groups=groups, tiled=True)  4.2 us
    pallas_call x1, Pallas kernels, outputs(): pl.pallas_call(functools.partial(output_kernel, replicas), in_specs=[pl.B...  3.82 us
    pallas_call x1, Pallas kernels, power_terms(): pl.pallas_call(power_kernel, out_shape=jax.ShapeDtypeStruct((rows, rank),...  3.72 us
  transfers between devices with their start and end apart: 2, of which 1 were waited for; matrix products, arithmetic and copies ran while one was open for 0% of the time, Pallas kernels for 11%

profile of v5, /device:TPU:2, one launch (start us, length us, event | category | flops | bytes accessed | tf_op | source)
XLA Modules:
  0.0 131.7 jit_solution(15014596798595834622)
XLA Ops:
  0.6 3.7 %shard_map.58 = f32[2048,128]{1,0:T(8,128)S(1)} custom-call(bf16[2048,384]{1,0:T(8,128)(2,1)} %grads_ref.5, bf16[2048,384]{1,0:T(8,128)(2,1)} %errors_ref.5, f32[384,128]{1,0:T(8,128)} %q_ref.1), custom_call_target="tpu_custom_call" | custom-call | tf_op jit(solution)/shard_map/pallas_call | solution.py:81
  4.4 4.6 %all_to_all.67 = f32[2,1024,128]{2,1,0:T(8,128)S(1)} all-to-all(f32[2,1024,128]{2,1,0:T(8,128)S(1)} %bitcast.10), channel_id=1, replica_groups=mesh['z'=16,'y'=4,'x'=4,'core'=2] {'core'}, dimensions={0} | all-to-all | bytes 2097152 | tf_op jit(solution)/shard_map/all_to_all | solution.py:266
  8.9 0.1 reduce_sum.54
  9.0 19.2 %all_to_all.68 = f32[16,64,128]{2,1,0:T(8,128)S(1)} all-to-all(f32[16,64,128]{2,1,0:T(8,128)S(1)} %bitcast.13), channel_id=1, replica_groups=mesh['z'=16,'y'=4,'x'=4,'core'=2] {'y','x'}, dimensions={0} | all-to-all | bytes 1048576 | tf_op jit(solution)/shard_map/all_to_all | solution.py:266
  28.3 10.2 %all_to_all.69 = f32[4,64,128]{2,1,0:T(8,128)S(1)} all-to-all(f32[4,64,128]{2,1,0:T(8,128)S(1)} %broadcast_in_dim.14), channel_id=1, replica_groups={{0,32,64,96},{128,160,192,224},{320,352,256,288},{448,480,384,416},{1,3..., dimensions={0} | all-to-all | bytes 262144 | tf_op jit(solution)/shard_map/all_to_all | solution.py:266
  38.5 23.4 %all_to_all.70 = f32[4,64,128]{2,1,0:T(8,128)S(1)} all-to-all(f32[4,64,128]{2,1,0:T(8,128)S(1)} %broadcast_in_dim.15), channel_id=1, replica_groups={{0,128,320,448},{32,160,352,480},{64,192,256,384},{96,224,288,416},{1,1..., dimensions={0} | all-to-all | bytes 262144 | tf_op jit(solution)/shard_map/all_to_all | solution.py:266
  62.0 13.1 %all_to_all.71 = f32[16,64,128]{2,1,0:T(8,128)S(1)} all-to-all(f32[16,64,128]{2,1,0:T(8,128)S(1)} %broadcast_in_dim.16), channel_id=1, replica_groups=mesh['z'=16,'y'=4,'x'=4,'core'=2] {'y','x'}, dimensions={0} | all-to-all | bytes 1048576 | tf_op jit(solution)/shard_map/all_to_all | solution.py:266
  75.1 0.0 copy-start
  75.1 0.0 copy-start.1
  75.1 0.1 broadcast_in_dim.18
  75.1 4.8 %all_to_all.72 = f32[2,1024,128]{2,1,0:T(8,128)S(1)} all-to-all(f32[2,1024,128]{2,1,0:T(8,128)S(1)} %broadcast_in_dim.18), channel_id=1, replica_groups=mesh['z'=16,'y'=4,'x'=4,'core'=2] {'core'}, dimensions={0} | all-to-all | bytes 2097152 | tf_op jit(solution)/shard_map/all_to_all | solution.py:266
  80.0 0.0 copy-start.2
  80.0 0.0 copy-done
  80.0 0.0 copy-done.1
  80.0 1.7 %shard_map.59 = f32[128,384]{1,0:T(8,128)} custom-call(bf16[2048,384]{1,0:T(8,128)(2,1)S(1)} %copy-done, bf16[2048,384]{1,0:T(8,128)(2,1)S(1)} %copy-done.1, f32[2048,128]{1,0:T(8,128)S(1)} %bitcast.7), custom_call_target="tpu_custom_call" | custom-call | tf_op jit(solution)/shard_map/pallas_call | solution.py:186
  81.7 0.0 copy-done.2
  81.7 3.5 %all-to-all-start.6 = ((f32[16,8,384]{2,1,0:T(8,128)}), f32[16,8,384]{2,1,0:T(8,128)S(1)}, u32[]{:S(2)}, u32[]{:S(2)}) async-start(f32[16,8,384]{2,1,0:T(8,128)} %bitcast.4), calls=%async_computation.6 | async-start | bytes 393216 | tf_op jit(solution)/shard_map/all_to_all | solution.py:266
  85.2 0.0 copy-start.3
  85.2 1.2 copy-done.3
  86.5 9.1 %shard_map.60 = (f32[128,128]{1,0:T(8,128)S(1)}, f32[128,128]{1,0:T(8,128)S(1)}) custom-call(f32[2048,128]{1,0:T(8,128)S(1)} %bitcast.8), custom_call_target="tpu_custom_call" | custom-call | flops 7000000000 | bytes 1048576 | tf_op jit(solution)/shard_map/pallas_call | solution.py:152
  95.6 0.0 all-to-all-done.6
  95.6 13.9 %all_to_all.73 = f32[4,8,384]{2,1,0:T(8,128)S(1)} all-to-all(f32[4,8,384]{2,1,0:T(8,128)S(1)} %broadcast_in_dim.19), channel_id=1, replica_groups={{0,128,320,448},{8,136,328,456},{16,144,336,464},{24,152,344,472},{32,1..., dimensions={0} | all-to-all | bytes 98304 | tf_op jit(solution)/shard_map/all_to_all | solution.py:266
  109.5 0.7 broadcast_in_dim.20
  110.2 8.0 %all-to-all-start.8 = ((f32[16,8,384]{2,1,0:T(8,128)}), f32[16,8,384]{2,1,0:T(8,128)S(1)}, u32[]{:S(2)}, u32[]{:S(2)}) async-start(f32[16,8,384]{2,1,0:T(8,128)} %broadcast_in_dim.20), calls=%async_computation.8 | async-start | bytes 393216 | tf_op jit(solution)/shard_map/all_to_all | solution.py:266
  118.2 0.0 copy-start.4
  118.3 5.2 %shard_map.61.maps_ref = f32[256,128]{1,0:T(8,128)S(1)} custom-call(f32[128,128]{1,0:T(8,128)S(1)} %get-tuple-element.18.first_ref, f32[128,128]{1,0:T(8,128)S(1)} %get-tuple-element.19.gram_ref), custom_call_target="tpu_custom_call" | custom-call | flops 7000000000 | bytes 1048576 | tf_op jit(solution)/shard_map/pallas_call | solution.py:165
  123.5 4.2 %all-to-all-done.8 = f32[16,8,384]{2,1,0:T(8,128)S(1)} async-done(((f32[16,8,384]{2,1,0:T(8,128)}), f32[16,8,384]{2,1,0:T(8,128)S(1)}, u32[]{:S(2)}, u32[]{:S(2)}) %all-to-all-start.8) | async-done | bytes 196640 | tf_op jit(solution)/shard_map/all_to_all | solution.py:266
  127.7 0.0 copy-done.4
  127.7 3.8 %shard_map.62 = (bf16[32,384]{1,0:T(8,128)(2,1)}, bf16[2048,384]{1,0:T(8,128)(2,1)}, f32[384,128]{1,0:T(8,128)}) custom-call(s32[1]{0:T(128)} %bitcast.5.own_ref, bf16[2048,384]{1,0:T(8,128)(2,1)} %grads_ref.5, bf16[2048,384]{1,0:T(8,128)(2,1)} %errors_ref.5, f32[2048,128]{1,0:T(8,128)S(1)} %bitcast.9, f32[256,128]{1,0:T(8,128)S(1)} %shard_map.61.maps_ref, ...), custom_call_target="tpu_custom_call" | custom-call | tf_op jit(solution)/shard_map/pallas_call | solution.py:241
  (9 shorter events, 0.2 us)
Async XLA Ops:
  75.1 4.9 %copy-start = (bf16[2048,384]{1,0:T(8,128)(2,1)S(1)}, bf16[2048,384]{1,0:T(8,128)(2,1)}, u32[]{:S(2)}) copy-start(bf16[2048,384]{1,0:T(8,128)(2,1)} %grads_ref.5) | copy-start | bytes 4718596
  75.1 4.9 %copy-start.1 = (bf16[2048,384]{1,0:T(8,128)(2,1)S(1)}, bf16[2048,384]{1,0:T(8,128)(2,1)}, u32[]{:S(2)}) copy-start(bf16[2048,384]{1,0:T(8,128)(2,1)} %errors_ref.5) | copy-start | bytes 4718596
  80.0 1.7 %copy-start.2 = (f32[2,1024,128]{2,1,0:T(8,128)}, f32[2,1024,128]{2,1,0:T(8,128)S(1)}, u32[]{:S(2)}) copy-start(f32[2,1024,128]{2,1,0:T(8,128)S(1)} %all_to_all.72) | copy-start | bytes 3145732
  81.7 13.9 %all-to-all-start.6 = ((f32[16,8,384]{2,1,0:T(8,128)}), f32[16,8,384]{2,1,0:T(8,128)S(1)}, u32[]{:S(2)}, u32[]{:S(2)}) async-start(f32[16,8,384]{2,1,0:T(8,128)} %bitcast.4), calls=%async_computation.6 | async-start | bytes 393216 | tf_op jit(solution)/shard_map/all_to_all | solution.py:266
  85.2 1.2 copy-start.3
  110.2 17.5 %all-to-all-start.8 = ((f32[16,8,384]{2,1,0:T(8,128)}), f32[16,8,384]{2,1,0:T(8,128)S(1)}, u32[]{:S(2)}, u32[]{:S(2)}) async-start(f32[16,8,384]{2,1,0:T(8,128)} %broadcast_in_dim.20), calls=%async_computation.8 | async-start | bytes 393216 | tf_op jit(solution)/shard_map/all_to_all | solution.py:266
  118.2 9.4 %copy-start.4 = (f32[2,1024,128]{2,1,0:T(8,128)S(1)}, f32[2,1024,128]{2,1,0:T(8,128)}, u32[]{:S(2)}) copy-start(f32[2,1024,128]{2,1,0:T(8,128)} %copy-done.2) | copy-start | bytes 3145732

commit v6 on v5

v6 whole, which is shorter than its diff:
```python
import functools

import jax
import jax.numpy as jnp
from jax import lax
from jax.experimental import pallas as pl
from jax.experimental.pallas import tpu as pltpu
from jax.sharding import Mesh, PartitionSpec as P

F32 = jnp.float32
BF16 = jnp.bfloat16
HIGHEST = lax.Precision.HIGHEST
ROWS_BY_ROWS = (((0,), (0,)), ((), ()))
LANES_BY_LANES = (((1,), (1,)), ((), ()))
WIDTH = 8
CHUNK = 512
VMEM_BYTES = 16 << 20
QR_COST = pl.CostEstimate(flops=7_000_000_000, bytes_accessed=1 << 20, transcendentals=0)

NEAR = 4
HALF_COST = pl.CostEstimate(flops=1_200_000_000, bytes_accessed=2 << 20, transcendentals=0)

DP = ("z", "y")
TENSOR = ("x", "core")


def pieces(values, count):
    parts = []
    for _ in range(count):
        part = values.astype(BF16)
        parts.append(part)
        values = values - part.astype(F32)
    return parts


def load(sources, buffers, sems, starts, size):
    def copy(k, n):
        rows = pl.ds(pl.multiple_of(starts[k], size), size)
        return pltpu.make_async_copy(sources[n].at[rows], buffers[n].at[pl.ds(k * size, size)], sems.at[k, n])

    for k in range(len(starts)):
        for n in range(len(sources)):
            copy(k, n).start()

    def wait(k):
        for n in range(len(sources)):
            copy(k, n).wait()

    return wait


def power_kernel(half_ref, grads_ref, errors_ref, q_ref, power_ref, held_g, held_e, held_q, split_ref, q_sem, sems):
    cols, rank = q_ref.shape
    rows = power_ref.shape[0]
    q_copy = pltpu.make_async_copy(q_ref, held_q, q_sem)
    q_copy.start()
    starts = [half_ref[0] * rows + k * CHUNK for k in range(rows // CHUNK)]
    wait = load((grads_ref, errors_ref), (held_g, held_e), sems, starts, CHUNK)
    q_copy.wait()
    for k, part in enumerate(pieces(held_q[...], 3)):
        split_ref[:cols, k * rank : (k + 1) * rank] = part
        split_ref[cols:, k * rank : (k + 1) * rank] = part
    for k in range(len(starts)):
        wait(k)
        chunk = slice(k * CHUNK, (k + 1) * CHUNK)
        both = jnp.concatenate([held_g[chunk, :], held_e[chunk, :]], axis=1)
        products = jnp.dot(both, split_ref[...], preferred_element_type=F32)
        power_ref[chunk, :] = products[:, :rank] + (products[:, rank : 2 * rank] + products[:, 2 * rank :])


IN_SMEM = pl.BlockSpec(memory_space=pltpu.SMEM)
IN_VMEM = pl.BlockSpec(memory_space=pltpu.VMEM)
IN_HBM = pl.BlockSpec(memory_space=pltpu.HBM)


def in_hbm(values):
    return pltpu.with_memory_space_constraint(values, pltpu.HBM)


def power_terms(grads, errors, q_init, half, keep):
    rows, cols = grads.shape[0] // 2, grads.shape[1]
    rank = q_init.shape[1]
    power = jax.ShapeDtypeStruct((rows, rank), F32)
    held = jax.ShapeDtypeStruct((rows, cols), BF16)
    return pl.pallas_call(
        power_kernel,
        out_shape=(power, held) if keep else power,
        in_specs=[IN_SMEM, IN_HBM, IN_HBM, IN_HBM],
        out_specs=(IN_VMEM,) * 2 if keep else IN_VMEM,
        scratch_shapes=[pltpu.VMEM((rows, cols), BF16)] * (1 if keep else 2)
        + [
            pltpu.VMEM((cols, rank), F32),
            pltpu.VMEM((2 * cols, 3 * rank), BF16),
            pltpu.SemaphoreType.DMA,
            pltpu.SemaphoreType.DMA((rows // CHUNK, 2)),
        ],
        compiler_params=pltpu.CompilerParams(vmem_limit_bytes=52 << 20),
        cost_estimate=HALF_COST,
    )(half, in_hbm(grads), in_hbm(errors), in_hbm(q_init))


def inverse_factor(gram, work_ref, inverse_ref):
    rank = gram.shape[0]
    lanes = lax.broadcasted_iota(jnp.int32, (WIDTH, rank), 1)
    subs = lax.broadcasted_iota(jnp.int32, (WIDTH, rank), 0)
    spread = lambda row: jnp.broadcast_to(row, (WIDTH, rank))
    work_ref[...] = gram
    for low in range(0, rank, WIDTH):
        own = work_ref[low : low + WIDTH, :]
        inside = (lanes >= low) & (lanes < low + WIDTH)
        columns = [spread(own[:, low + k : low + k + 1]) for k in range(WIDTH)]
        block = jnp.where(inside, (lanes - low == subs).astype(F32), own)
        forward = jnp.zeros((WIDTH, rank), F32)
        pivots = jnp.ones((WIDTH, rank), F32)
        reciprocals = jnp.zeros((WIDTH, rank), F32)
        for j in range(WIDTH):
            heads = [spread(column[j : j + 1, :]) for column in columns[j:]]
            row = spread(block[j : j + 1, :])
            forward = jnp.where(subs == j, row, forward)
            pivots = jnp.where(subs == j, heads[0], pivots)
            reciprocal = 1.0 / heads[0]
            reciprocals = jnp.where(subs == j, reciprocal, reciprocals)
            factor = jnp.where(subs == j, 0.0, columns[j] * reciprocal)
            for k in range(j + 1, WIDTH):
                columns[k] = columns[k] - factor * heads[k - j]
            block = block - factor * row
        inverse_ref[low : low + WIDTH, :] = jnp.where(lanes < low + WIDTH, forward * lax.rsqrt(pivots), 0.0)
        block = block * reciprocals
        solved = [spread(block[k : k + 1, :]) for k in range(WIDTH)]
        for at in range(low + WIDTH, rank, WIDTH):
            rest = work_ref[at : at + WIDTH, :]
            terms = [spread(rest[:, low + k : low + k + 1]) * solved[k] for k in range(WIDTH)]
            while len(terms) > 1:
                terms = [a + b for a, b in zip(terms[::2], terms[1::2], strict=True)]
            work_ref[at : at + WIDTH, :] = jnp.where(inside, 0.0, rest) - terms[0]


def gram_of(halves):
    terms = [
        lax.dot_general(half, half, ROWS_BY_ROWS, precision=HIGHEST, preferred_element_type=F32) for half in halves
    ]
    return terms[0] + terms[1]


def first_pass_kernel(kept_ref, other_ref, first_ref, work_ref):
    inverse_factor(gram_of([kept_ref[...], other_ref[...]]), work_ref, first_ref)


def second_pass_kernel(kept_ref, other_ref, first_ref, maps_ref, work_ref, second_ref):
    rank = first_ref.shape[0]
    first = [
        lax.dot_general(half[...], first_ref[...], LANES_BY_LANES, precision=HIGHEST, preferred_element_type=F32)
        for half in (kept_ref, other_ref)
    ]
    inverse_factor(gram_of(first), work_ref, second_ref)
    both = jnp.dot(second_ref[...], first_ref[...], precision=HIGHEST, preferred_element_type=F32)
    maps_ref[:rank, :] = both
    maps_ref[rank:, :] = lax.dot_general(both, both, ROWS_BY_ROWS, precision=HIGHEST, preferred_element_type=F32)


def first_pass(power):
    square = (power[0].shape[1],) * 2
    return pl.pallas_call(
        first_pass_kernel,
        out_shape=jax.ShapeDtypeStruct(square, F32),
        in_specs=[IN_VMEM, IN_VMEM],
        out_specs=IN_VMEM,
        scratch_shapes=[pltpu.VMEM(square, F32)],
        compiler_params=pltpu.CompilerParams(vmem_limit_bytes=32 << 20),
        cost_estimate=QR_COST,
    )(*power)


def second_pass(power, first):
    square = first.shape
    return pl.pallas_call(
        second_pass_kernel,
        out_shape=jax.ShapeDtypeStruct((2 * square[0], square[1]), F32),
        in_specs=[IN_VMEM] * 3,
        out_specs=IN_VMEM,
        scratch_shapes=[pltpu.VMEM(square, F32)] * 2,
        compiler_params=pltpu.CompilerParams(vmem_limit_bytes=32 << 20),
        cost_estimate=QR_COST,
    )(*power, first)


def power_by_merged(power, grads, errors):
    rank, cols = power.shape[1], grads.shape[1]
    split = jnp.concatenate(pieces(power, 2), axis=1)
    both = jnp.concatenate([grads, errors], axis=1)
    products = lax.dot_general(split, both, ROWS_BY_ROWS, preferred_element_type=F32)
    products = products[:, :cols] + products[:, cols:]
    return products[:rank, :] + products[rank:, :]


def kept_factor_kernel(half_ref, grads_ref, errors_ref, power_ref, terms_ref, other_ref, held_g, held_e, sems, other_sem):
    count = power_ref.shape[0]
    wait = load((grads_ref, errors_ref), (held_g, held_e), sems, [half_ref[0] * count], count)
    rows = pl.ds(pl.multiple_of((1 - half_ref[0]) * count, count), count)
    other = pltpu.make_async_copy(errors_ref.at[rows], other_ref, other_sem)
    other.start()
    wait(0)
    terms_ref[...] = power_by_merged(power_ref[...], held_g[...], held_e[...])
    other.wait()


def other_factor_kernel(grads_ref, errors_ref, power_ref, before_ref, terms_ref):
    terms_ref[...] = before_ref[...] + power_by_merged(power_ref[...], grads_ref[...], errors_ref[...])


def kept_factor_terms(grads, errors, power, half):
    rows, rank = power.shape
    cols = grads.shape[1]
    return pl.pallas_call(
        kept_factor_kernel,
        out_shape=(jax.ShapeDtypeStruct((rank, cols), F32), jax.ShapeDtypeStruct((rows, cols), BF16)),
        in_specs=[IN_SMEM, IN_HBM, IN_HBM, IN_VMEM],
        out_specs=(IN_VMEM, IN_VMEM),
        scratch_shapes=[pltpu.VMEM((rows, cols), BF16)] * 2 + [pltpu.SemaphoreType.DMA((1, 2)), pltpu.SemaphoreType.DMA],
        compiler_params=pltpu.CompilerParams(vmem_limit_bytes=32 << 20),
        cost_estimate=HALF_COST,
    )(half, in_hbm(grads), in_hbm(errors), power)


def other_factor_terms(grads, errors, power, before):
    return pl.pallas_call(
        other_factor_kernel,
        out_shape=jax.ShapeDtypeStruct(before.shape, F32),
        in_specs=[IN_VMEM] * 4,
        out_specs=IN_VMEM,
        compiler_params=pltpu.CompilerParams(vmem_limit_bytes=32 << 20),
        cost_estimate=HALF_COST,
    )(grads, errors, power, before)


def output_kernel(replicas, place_ref, grads_ref, errors_ref, kept_ref, other_ref, maps_ref, terms_ref,
                  avg_ref, new_ref, q_ref, held_g, held_e, held_new, held_avg, held_q, sems, out_sems, avg_sem, q_sem):
    rank = kept_ref.shape[1]
    count = kept_ref.shape[0]
    share = avg_ref.shape[0]
    kept_half, own = place_ref[0], place_ref[1]
    starts = [kept_half * count, (1 - kept_half) * count]
    wait = load((grads_ref, errors_ref), (held_g, held_e), sems, starts, count)
    writes = []

    def write(held, out, sem):
        writes.append(pltpu.make_async_copy(held, out, sem))
        writes[-1].start()

    def left(values):
        high, low = pieces(values, 2)
        return jnp.concatenate([high, high, low], axis=1)

    def right(values):
        high, low = pieces(values, 2)
        return jnp.concatenate([high, low, high], axis=0)

    def product(values, stacked):
        return jnp.dot(left(values), stacked, preferred_element_type=F32)

    terms = right(terms_ref[...] * (1.0 / replicas))
    mapped = right(product(maps_ref[rank:, :], terms))
    for k, power_ref in enumerate((kept_ref, other_ref)):
        wait(k)
        rows = slice(k * count, (k + 1) * count)
        merged = held_g[rows, :].astype(F32) + held_e[rows, :].astype(F32)
        held_new[rows, :] = (merged - product(power_ref[...], mapped)).astype(BF16)
        out = pl.ds(pl.multiple_of(starts[k], count), count)
        write(held_new.at[pl.ds(k * count, count)], new_ref.at[out], out_sems.at[k])
        if k == 0:
            per_half = count // share
            rows = pl.ds(pl.multiple_of(lax.rem(own, per_half) * share, share), share)
            here = jnp.broadcast_to(own // per_half == kept_half, (share, rank))
            held_avg[...] = product(jnp.where(here, kept_ref[rows, :], other_ref[rows, :]), mapped).astype(BF16)
            write(held_avg, avg_ref, avg_sem)
            held_q[...] = product(maps_ref[:rank, :], terms).T
            write(held_q, q_ref, q_sem)
    for copy in writes:
        copy.wait()


def outputs(grads, errors, power, maps, terms, replicas, place):
    rows, cols = grads.shape
    rank = power[0].shape[1]
    share = rows // replicas
    return pl.pallas_call(
        functools.partial(output_kernel, replicas),
        in_specs=[IN_SMEM, IN_HBM, IN_HBM] + [IN_VMEM] * 4,
        out_specs=(IN_HBM, IN_HBM, IN_HBM),
        out_shape=(
            jax.ShapeDtypeStruct((share, cols), BF16),
            jax.ShapeDtypeStruct((rows, cols), BF16),
            jax.ShapeDtypeStruct((cols, rank), F32),
        ),
        scratch_shapes=[
            pltpu.VMEM((rows, cols), BF16),
            pltpu.VMEM((rows, cols), BF16),
            pltpu.VMEM((rows, cols), BF16),
            pltpu.VMEM((share, cols), BF16),
            pltpu.VMEM((cols, rank), F32),
            pltpu.SemaphoreType.DMA((2, 2)),
            pltpu.SemaphoreType.DMA((2,)),
            pltpu.SemaphoreType.DMA,
            pltpu.SemaphoreType.DMA,
        ],
        compiler_params=pltpu.CompilerParams(vmem_limit_bytes=52 << 20),
    )(place, in_hbm(grads), in_hbm(errors), *power, maps, terms)


def exchange(values, axes, groups):
    return lax.all_to_all(values, axes, 0, 0, axis_index_groups=groups, tiled=True)


def members(axes, groups):
    return lax.axis_size(axes) if groups is None else len(groups[0])


def scatter_sum(values, axes, groups=None):
    count = members(axes, groups)
    shares = exchange(values, axes, groups)
    return shares.reshape(count, values.shape[0] // count, values.shape[1]).sum(axis=0)


def gather(values, axes, groups=None):
    copies = jnp.broadcast_to(values[None], (members(axes, groups), *values.shape)).reshape(-1, values.shape[1])
    return exchange(copies, axes, groups)


def exchange_sum(values, axes, groups):
    return gather(values, axes, groups).reshape(members(axes, groups), *values.shape).sum(axis=0)


def z_groups(length, width):
    blocks = length // NEAR

    def device(block, share, y):
        turn = NEAR // 2 if 2 * block >= blocks else 0
        return (block * NEAR + (share + turn) % NEAR) * width + y

    shares = [(share, y) for share in range(NEAR) for y in range(width)]
    near = [[device(block, *share) for share in shares] for block in range(blocks)]
    far = [[device(block, *share) for block in range(blocks)] for share in shares]
    return near, far


def swap(values):
    return lax.ppermute(values, "core", [(0, 1), (1, 0)])


def body(grads, errors, q_init):
    replicas = lax.axis_size(DP)
    half = lax.axis_index("core").reshape(1)
    sent, other_grads = power_terms(grads, errors, q_init, 1 - half, keep=True)
    received = swap(sent)
    power = power_terms(grads, errors, q_init, half, keep=False) + received

    near, far = z_groups(lax.axis_size("z"), 1)
    power = scatter_sum(power, ("y", "x"))
    power = exchange_sum(power, "z", near)
    power = exchange_sum(power, "z", far)
    power = gather(power, ("y", "x"))
    power = (power, swap(power))

    near, far = z_groups(lax.axis_size("z"), lax.axis_size("y"))
    terms, other_errors = kept_factor_terms(grads, errors, power[0], half)
    terms = other_factor_terms(other_grads, other_errors, power[1], terms)
    first = first_pass(power)
    place = jnp.concatenate([half, lax.axis_index(DP).reshape(1)])
    terms = scatter_sum(terms, DP, near)
    terms, first, place = lax.optimization_barrier((terms, first, place))
    terms = exchange_sum(terms, DP, far)
    terms, first = lax.optimization_barrier((terms, first))
    maps = second_pass(power, first)
    terms = gather(terms, DP, near)
    return outputs(grads, errors, power, maps, terms, replicas, place)


def solution(mesh):
    fine = Mesh(mesh.devices.reshape(16, 4, 4, 2), ("z", "y", "x", "core"))
    placed = (P(DP, TENSOR), P(DP, TENSOR), P(TENSOR, None))
    return jax.shard_map(
        body,
        mesh=fine,
        in_specs=placed,
        out_specs=(P(DP, TENSOR), P(DP, TENSOR), P(TENSOR, None)),
        check_vma=False,
    )
```

time: 132 us -> 127 us (0.962)
  blocking collectives: 89.2 us -> 79.8 us
  waiting for transfers between devices: 4.2 us -> 7.1 us
  Pallas kernels: 23.6 us -> 25.6 us
    all_to_all x7 -> x5, blocking collectives: 89.2 us -> 79.8 us  [exchange(): lax.all_to_all(values, axes, 0, 0, axis_index_groups=groups, tiled=True)]
    ppermute x0 -> x2, starting transfers between devices: none -> 3.83 us  [swap(): return lax.ppermute(values, 'core', [(0, 1), (1, 0)])]
    all_to_all x2, starting transfers between devices: 11.5 us -> 7.86 us  [exchange(): lax.all_to_all(values, axes, 0, 0, axis_index_groups=groups, tiled=True)]
    all_to_all x2, waiting for transfers between devices: 4.2 us -> 7.1 us  [exchange(): lax.all_to_all(values, axes, 0, 0, axis_index_groups=groups, tiled=True)]
    pallas_call x5 -> x7, Pallas kernels: 23.6 us -> 25.6 us  [the longest x1 7.27 us: second_pass(): pl.pallas_call(second_pass_kernel, out_shape=jax.ShapeDtypeStruct((2 * sq...]
  transfers between devices with their start and end apart: 2 -> 4, of which waited for: 1 -> 2; matrix products, arithmetic and copies ran while one was open for 0% -> 0% of each run, Pallas kernels for 11% -> 14%
where the time goes in v6:
time: 127 us; the launch traced here: 126 us
  blocking collectives  79.8 us (63%)
  Pallas kernels  25.6 us (20%)
  starting transfers between devices  11.7 us (9%)
  waiting for transfers between devices  7.1 us (6%)
    all_to_all x5, blocking collectives, exchange(): lax.all_to_all(values, axes, 0, 0, axis_index_groups=groups, tiled=True)  79.8 us
    all_to_all x2, starting transfers between devices, exchange(): lax.all_to_all(values, axes, 0, 0, axis_index_groups=groups, tiled=True)  7.86 us
    pallas_call x1, Pallas kernels, second_pass(): pl.pallas_call(second_pass_kernel, out_shape=jax.ShapeDtypeStruct((2 * sq...  7.27 us
    all_to_all x2, waiting for transfers between devices, exchange(): lax.all_to_all(values, axes, 0, 0, axis_index_groups=groups, tiled=True)  7.1 us
    pallas_call x1, Pallas kernels, first_pass(): pl.pallas_call(first_pass_kernel, out_shape=jax.ShapeDtypeStruct(square,...  5.52 us
    pallas_call x2, Pallas kernels, power_terms(): pl.pallas_call(power_kernel, out_shape=(power, held) if keep else power,...  5.13 us
    pallas_call x1, Pallas kernels, outputs(): pl.pallas_call(functools.partial(output_kernel, replicas), in_specs=[IN_S...  4.36 us
    ppermute x2, starting transfers between devices, swap(): return lax.ppermute(values, 'core', [(0, 1), (1, 0)])  3.83 us
  transfers between devices with their start and end apart: 4, of which 2 were waited for; matrix products, arithmetic and copies ran while one was open for 0% of the time, Pallas kernels for 14%

profile of v6, /device:TPU:2, one launch (start us, length us, event | category | flops | bytes accessed | tf_op | source)
XLA Modules:
  0.0 126.1 jit_solution(3177911986585500283)
XLA Ops:
  0.6 2.6 %shard_map.58 = (f32[1024,128]{1,0:T(8,128)S(1)}, bf16[1024,384]{1,0:T(8,128)(2,1)S(1)}) custom-call(s32[1]{0:T(128)S(6)} %sub.3.half_ref, bf16[2048,384]{1,0:T(8,128)(2,1)} %grads_ref.7, bf16[2048,384]{1,0:T(8,128)(2,1)} %errors_ref.7, f32[384,128]{1,0:T(8,128)} %q_ref.3), custom_call_target="tpu_custom_call" | custom-call | flops 1200000000 | bytes 2097152 | tf_op jit(solution)/shard_map/pallas_call | solution.py:85
  3.2 1.9 %collective-permute-start = (f32[1024,128]{1,0:T(8,128)S(1)}, f32[1024,128]{1,0:T(8,128)S(1)}, u32[]{:S(2)}, u32[]{:S(2)}) collective-permute-start(f32[1024,128]{1,0:T(8,128)S(1)} %get-tuple-element.13), channel_id=1, source_target_pairs={{0,1},{1,0},{2,3},{3,2},{4,5},{5,4},{6,7},{7,6},{8,9},{9,8},{10,11... | collective-permute-start | bytes 1572872 | tf_op jit(solution)/shard_map/ppermute | solution.py:347
  5.1 2.6 %shard_map.59 = f32[1024,128]{1,0:T(8,128)S(1)} custom-call(s32[1]{0:T(128)} %bitcast.half_ref, bf16[2048,384]{1,0:T(8,128)(2,1)} %grads_ref.7, bf16[2048,384]{1,0:T(8,128)(2,1)} %errors_ref.7, f32[384,128]{1,0:T(8,128)} %q_ref.3), custom_call_target="tpu_custom_call" | custom-call | flops 1200000000 | bytes 2097152 | tf_op jit(solution)/shard_map/pallas_call | solution.py:85
  7.7 0.0 collective-permute-done
  7.7 0.1 add.6
  7.8 19.5 %all_to_all.52 = f32[16,64,128]{2,1,0:T(8,128)S(1)} all-to-all(f32[16,64,128]{2,1,0:T(8,128)S(1)} %bitcast.12), channel_id=1, replica_groups=mesh['z'=16,'y'=4,'x'=4,'core'=2] {'y','x'}, dimensions={0} | all-to-all | bytes 1048576 | tf_op jit(solution)/shard_map/all_to_all | solution.py:311
  27.4 10.2 %all_to_all.53 = f32[4,64,128]{2,1,0:T(8,128)S(1)} all-to-all(f32[4,64,128]{2,1,0:T(8,128)S(1)} %broadcast_in_dim.10), channel_id=1, replica_groups={{0,32,64,96},{128,160,192,224},{320,352,256,288},{448,480,384,416},{1,3..., dimensions={0} | all-to-all | bytes 262144 | tf_op jit(solution)/shard_map/all_to_all | solution.py:311
  37.6 23.4 %all_to_all.54 = f32[4,64,128]{2,1,0:T(8,128)S(1)} all-to-all(f32[4,64,128]{2,1,0:T(8,128)S(1)} %broadcast_in_dim.11), channel_id=1, replica_groups={{0,128,320,448},{32,160,352,480},{64,192,256,384},{96,224,288,416},{1,1..., dimensions={0} | all-to-all | bytes 262144 | tf_op jit(solution)/shard_map/all_to_all | solution.py:311
  61.1 13.0 %all_to_all.55 = f32[16,64,128]{2,1,0:T(8,128)S(1)} all-to-all(f32[16,64,128]{2,1,0:T(8,128)S(1)} %broadcast_in_dim.12), channel_id=1, replica_groups=mesh['z'=16,'y'=4,'x'=4,'core'=2] {'y','x'}, dimensions={0} | all-to-all | bytes 1048576 | tf_op jit(solution)/shard_map/all_to_all | solution.py:311
  74.1 1.9 %collective-permute-start.1 = (f32[1024,128]{1,0:T(8,128)S(1)}, f32[1024,128]{1,0:T(8,128)S(1)}, u32[]{:S(2)}, u32[]{:S(2)}) collective-permute-start(f32[1024,128]{1,0:T(8,128)S(1)} %bitcast.6), channel_id=1, source_target_pairs={{0,1},{1,0},{2,3},{3,2},{4,5},{5,4},{6,7},{7,6},{8,9},{9,8},{10,11... | collective-permute-start | bytes 1572872 | tf_op jit(solution)/shard_map/ppermute | solution.py:347
  76.0 2.0 %shard_map.60 = (f32[128,384]{1,0:T(8,128)S(1)}, bf16[1024,384]{1,0:T(8,128)(2,1)S(1)}) custom-call(s32[1]{0:T(128)} %bitcast.half_ref, bf16[2048,384]{1,0:T(8,128)(2,1)} %grads_ref.7, bf16[2048,384]{1,0:T(8,128)(2,1)} %errors_ref.7, f32[1024,128]{1,0:T(8,128)S(1)} %bitcast.7), custom_call_target="tpu_custom_call" | custom-call | flops 1200000000 | bytes 2097152 | tf_op jit(solution)/shard_map/pallas_call | solution.py:214
  78.1 0.0 collective-permute-done.1.power_ref.other_ref
  78.1 1.3 %shard_map.61 = f32[128,384]{1,0:T(8,128)} custom-call(bf16[1024,384]{1,0:T(8,128)(2,1)S(1)} %get-tuple-element.12.grads_ref, bf16[1024,384]{1,0:T(8,128)(2,1)S(1)} %get-tuple-element.14.errors_ref, f32[1024,128]{1,0:T(8,128)S(1)} %collective-permute-done.1.power_ref.other_ref, f32[128,384]{1,0:T(8,128)S(1)} %get-tuple-element.15.before_ref), custom_call_target="tpu_custom_call" | custom-call | flops 1200000000 | bytes 2097152 | tf_op jit(solution)/shard_map/pallas_call | solution.py:226
  79.4 3.5 %all-to-all-start.4 = ((f32[16,8,384]{2,1,0:T(8,128)}), f32[16,8,384]{2,1,0:T(8,128)S(1)}, u32[]{:S(2)}, u32[]{:S(2)}) async-start(f32[16,8,384]{2,1,0:T(8,128)} %bitcast.3), calls=%async_computation.4 | async-start | bytes 393216 | tf_op jit(solution)/shard_map/all_to_all | solution.py:311
  82.9 0.1 pad_add_fusion.place_ref
  83.0 5.5 %shard_map.62.first_ref = f32[128,128]{1,0:T(8,128)S(1)} custom-call(f32[1024,128]{1,0:T(8,128)S(1)} %bitcast.8, f32[1024,128]{1,0:T(8,128)S(1)} %collective-permute-done.1.power_ref.other_ref), custom_call_target="tpu_custom_call" | custom-call | flops 7000000000 | bytes 1048576 | tf_op jit(solution)/shard_map/pallas_call | solution.py:163
  88.5 4.9 %all-to-all-done.4 = f32[16,8,384]{2,1,0:T(8,128)S(1)} async-done(((f32[16,8,384]{2,1,0:T(8,128)}), f32[16,8,384]{2,1,0:T(8,128)S(1)}, u32[]{:S(2)}, u32[]{:S(2)}) %all-to-all-start.4) | async-done | bytes 196640 | tf_op jit(solution)/shard_map/all_to_all | solution.py:311
  93.5 13.6 %all_to_all.56 = f32[4,8,384]{2,1,0:T(8,128)S(1)} all-to-all(f32[4,8,384]{2,1,0:T(8,128)S(1)} %broadcast_in_dim.13), channel_id=1, replica_groups={{0,128,320,448},{8,136,328,456},{16,144,336,464},{24,152,344,472},{32,1..., dimensions={0} | all-to-all | bytes 98304 | tf_op jit(solution)/shard_map/all_to_all | solution.py:311
  107.1 0.7 broadcast_in_dim.14
  107.8 4.3 %all-to-all-start.6 = ((f32[16,8,384]{2,1,0:T(8,128)}), f32[16,8,384]{2,1,0:T(8,128)S(1)}, u32[]{:S(2)}, u32[]{:S(2)}) async-start(f32[16,8,384]{2,1,0:T(8,128)} %broadcast_in_dim.14), calls=%async_computation.6 | async-start | bytes 393216 | tf_op jit(solution)/shard_map/all_to_all | solution.py:311
  112.2 7.3 %shard_map.63.maps_ref = f32[256,128]{1,0:T(8,128)S(1)} custom-call(f32[1024,128]{1,0:T(8,128)S(1)} %bitcast.9, f32[1024,128]{1,0:T(8,128)S(1)} %collective-permute-done.1.power_ref.other_ref, f32[128,128]{1,0:T(8,128)S(1)} %shard_map.62.first_ref), custom_call_target="tpu_custom_call" | custom-call | flops 7000000000 | bytes 1048576 | tf_op jit(solution)/shard_map/pallas_call | solution.py:176
  119.4 2.2 %all-to-all-done.6 = f32[16,8,384]{2,1,0:T(8,128)S(1)} async-done(((f32[16,8,384]{2,1,0:T(8,128)}), f32[16,8,384]{2,1,0:T(8,128)S(1)}, u32[]{:S(2)}, u32[]{:S(2)}) %all-to-all-start.6) | async-done | bytes 196640 | tf_op jit(solution)/shard_map/all_to_all | solution.py:311
  121.6 4.4 %shard_map.64 = (bf16[32,384]{1,0:T(8,128)(2,1)}, bf16[2048,384]{1,0:T(8,128)(2,1)}, f32[384,128]{1,0:T(8,128)}) custom-call(s32[2]{0:T(128)S(1)} %pad_add_fusion.place_ref, bf16[2048,384]{1,0:T(8,128)(2,1)} %grads_ref.7, bf16[2048,384]{1,0:T(8,128)(2,1)} %errors_ref.7, f32[1024,128]{1,0:T(8,128)S(1)} %bitcast.10, ...), custom_call_target="tpu_custom_call" | custom-call | tf_op jit(solution)/shard_map/pallas_call | solution.py:286
  (9 shorter events, 0.2 us)
Async XLA Ops:
  3.2 4.5 %collective-permute-start = (f32[1024,128]{1,0:T(8,128)S(1)}, f32[1024,128]{1,0:T(8,128)S(1)}, u32[]{:S(2)}, u32[]{:S(2)}) collective-permute-start(f32[1024,128]{1,0:T(8,128)S(1)} %get-tuple-element.13), channel_id=1, source_target_pairs={{0,1},{1,0},{2,3},{3,2},{4,5},{5,4},{6,7},{7,6},{8,9},{9,8},{10,11... | collective-permute-start | bytes 1572872 | tf_op jit(solution)/shard_map/ppermute | solution.py:347
  74.1 4.0 %collective-permute-start.1 = (f32[1024,128]{1,0:T(8,128)S(1)}, f32[1024,128]{1,0:T(8,128)S(1)}, u32[]{:S(2)}, u32[]{:S(2)}) collective-permute-start(f32[1024,128]{1,0:T(8,128)S(1)} %bitcast.6), channel_id=1, source_target_pairs={{0,1},{1,0},{2,3},{3,2},{4,5},{5,4},{6,7},{7,6},{8,9},{9,8},{10,11... | collective-permute-start | bytes 1572872 | tf_op jit(solution)/shard_map/ppermute | solution.py:347
  79.4 14.1 %all-to-all-start.4 = ((f32[16,8,384]{2,1,0:T(8,128)}), f32[16,8,384]{2,1,0:T(8,128)S(1)}, u32[]{:S(2)}, u32[]{:S(2)}) async-start(f32[16,8,384]{2,1,0:T(8,128)} %bitcast.3), calls=%async_computation.4 | async-start | bytes 393216 | tf_op jit(solution)/shard_map/all_to_all | solution.py:311
  107.8 13.8 %all-to-all-start.6 = ((f32[16,8,384]{2,1,0:T(8,128)}), f32[16,8,384]{2,1,0:T(8,128)S(1)}, u32[]{:S(2)}, u32[]{:S(2)}) async-start(f32[16,8,384]{2,1,0:T(8,128)} %broadcast_in_dim.14), calls=%async_computation.6 | async-start | bytes 393216 | tf_op jit(solution)/shard_map/all_to_all | solution.py:311

commit v7 on v6

--- a/solution.py
+++ b/solution.py
@@ -12,7 +12,7 @@
 HIGHEST = lax.Precision.HIGHEST
 ROWS_BY_ROWS = (((0,), (0,)), ((), ()))
 LANES_BY_LANES = (((1,), (1,)), ((), ()))
-WIDTH = 8
+WIDTH = 16
 CHUNK = 512
 VMEM_BYTES = 16 << 20
 QR_COST = pl.CostEstimate(flops=7_000_000_000, bytes_accessed=1 << 20, transcendentals=0)
@@ -33,6 +33,10 @@
     return parts
 
 
+def half_rows(half, count):
+    return pl.ds(pl.multiple_of(half * count, count), count)
+
+
 def load(sources, buffers, sems, starts, size):
     def copy(k, n):
         rows = pl.ds(pl.multiple_of(starts[k], size), size)
@@ -49,23 +53,43 @@
     return wait
 
 
-def power_kernel(half_ref, grads_ref, errors_ref, q_ref, power_ref, held_g, held_e, held_q, split_ref, q_sem, sems):
-    cols, rank = q_ref.shape
+def power_product(grads, errors, split):
+    rank = split.shape[1] // 3
+    products = jnp.dot(jnp.concatenate([grads, errors], axis=1), split, preferred_element_type=F32)
+    return products[:, :rank] + (products[:, rank : 2 * rank] + products[:, 2 * rank :])
+
+
+def split_q(q, split_ref):
+    cols, rank = q.shape
+    for k, part in enumerate(pieces(q, 3)):
+        split_ref[:cols, k * rank : (k + 1) * rank] = part
+        split_ref[cols:, k * rank : (k + 1) * rank] = part
+
+
+def sent_power_kernel(half_ref, grads_ref, errors_ref, q_ref, power_ref, own_g,
+                      other_g, other_e, held_q, split_ref, q_sem, sems, own_sem):
     rows = power_ref.shape[0]
     q_copy = pltpu.make_async_copy(q_ref, held_q, q_sem)
     q_copy.start()
-    starts = [half_ref[0] * rows + k * CHUNK for k in range(rows // CHUNK)]
-    wait = load((grads_ref, errors_ref), (held_g, held_e), sems, starts, CHUNK)
+    starts = [(1 - half_ref[0]) * rows + k * CHUNK for k in range(rows // CHUNK)]
+    wait = load((grads_ref, errors_ref), (other_g, other_e), sems, starts, CHUNK)
+    own = pltpu.make_async_copy(grads_ref.at[half_rows(half_ref[0], rows)], own_g, own_sem)
+    own.start()
     q_copy.wait()
-    for k, part in enumerate(pieces(held_q[...], 3)):
-        split_ref[:cols, k * rank : (k + 1) * rank] = part
-        split_ref[cols:, k * rank : (k + 1) * rank] = part
+    split_q(held_q[...], split_ref)
     for k in range(len(starts)):
         wait(k)
         chunk = slice(k * CHUNK, (k + 1) * CHUNK)
-        both = jnp.concatenate([held_g[chunk, :], held_e[chunk, :]], axis=1)
-        products = jnp.dot(both, split_ref[...], preferred_element_type=F32)
-        power_ref[chunk, :] = products[:, :rank] + (products[:, rank : 2 * rank] + products[:, 2 * rank :])
+        power_ref[chunk, :] = power_product(other_g[chunk, :], other_e[chunk, :], split_ref[...])
+    own.wait()
+
+
+def kept_power_kernel(half_ref, grads_ref, errors_ref, q_ref, power_ref, own_e, split_ref, sem):
+    own = pltpu.make_async_copy(errors_ref.at[half_rows(half_ref[0], power_ref.shape[0])], own_e, sem)
+    own.start()
+    split_q(q_ref[...], split_ref)
+    own.wait()
+    power_ref[...] = power_product(grads_ref[...], own_e[...], split_ref[...])
 
 
 IN_SMEM = pl.BlockSpec(memory_space=pltpu.SMEM)
@@ -77,26 +101,45 @@
     return pltpu.with_memory_space_constraint(values, pltpu.HBM)
 
 
-def power_terms(grads, errors, q_init, half, keep):
+def sent_power_terms(grads, errors, q_init, half):
     rows, cols = grads.shape[0] // 2, grads.shape[1]
     rank = q_init.shape[1]
-    power = jax.ShapeDtypeStruct((rows, rank), F32)
     held = jax.ShapeDtypeStruct((rows, cols), BF16)
     return pl.pallas_call(
-        power_kernel,
-        out_shape=(power, held) if keep else power,
+        sent_power_kernel,
+        out_shape=(jax.ShapeDtypeStruct((rows, rank), F32), held),
         in_specs=[IN_SMEM, IN_HBM, IN_HBM, IN_HBM],
-        out_specs=(IN_VMEM,) * 2 if keep else IN_VMEM,
-        scratch_shapes=[pltpu.VMEM((rows, cols), BF16)] * (1 if keep else 2)
-        + [
+        out_specs=(IN_VMEM,) * 2,
+        scratch_shapes=[
+            pltpu.VMEM((rows, cols), BF16),
+            pltpu.VMEM((rows, cols), BF16),
             pltpu.VMEM((cols, rank), F32),
             pltpu.VMEM((2 * cols, 3 * rank), BF16),
             pltpu.SemaphoreType.DMA,
             pltpu.SemaphoreType.DMA((rows // CHUNK, 2)),
+            pltpu.SemaphoreType.DMA,
         ],
         compiler_params=pltpu.CompilerParams(vmem_limit_bytes=52 << 20),
         cost_estimate=HALF_COST,
     )(half, in_hbm(grads), in_hbm(errors), in_hbm(q_init))
+
+
+def kept_power_terms(own_grads, errors, q_init, half):
+    cols, rank = q_init.shape
+    rows = own_grads.shape[0]
+    return pl.pallas_call(
+        kept_power_kernel,
+        out_shape=jax.ShapeDtypeStruct((rows, rank), F32),
+        in_specs=[IN_SMEM, IN_VMEM, IN_HBM, IN_VMEM],
+        out_specs=IN_VMEM,
+        scratch_shapes=[
+            pltpu.VMEM((rows, cols), BF16),
+            pltpu.VMEM((2 * cols, 3 * rank), BF16),
+            pltpu.SemaphoreType.DMA,
+        ],
+        compiler_params=pltpu.CompilerParams(vmem_limit_bytes=32 << 20),
+        cost_estimate=HALF_COST,
+    )(half, own_grads, in_hbm(errors), q_init)
 
 
 def inverse_factor(gram, work_ref, inverse_ref):
@@ -146,8 +189,10 @@
     inverse_factor(gram_of([kept_ref[...], other_ref[...]]), work_ref, first_ref)
 
 
-def second_pass_kernel(kept_ref, other_ref, first_ref, maps_ref, work_ref, second_ref):
+def second_pass_kernel(kept_ref, other_ref, first_ref, grads_ref, maps_ref, held_ref, work_ref, second_ref, sem):
     rank = first_ref.shape[0]
+    held = pltpu.make_async_copy(grads_ref, held_ref, sem)
+    held.start()
     first = [
         lax.dot_general(half[...], first_ref[...], LANES_BY_LANES, precision=HIGHEST, preferred_element_type=F32)
         for half in (kept_ref, other_ref)
@@ -156,6 +201,7 @@
     both = jnp.dot(second_ref[...], first_ref[...], precision=HIGHEST, preferred_element_type=F32)
     maps_ref[:rank, :] = both
     maps_ref[rank:, :] = lax.dot_general(both, both, ROWS_BY_ROWS, precision=HIGHEST, preferred_element_type=F32)
+    held.wait()
 
 
 def first_pass(power):
@@ -171,17 +217,20 @@
     )(*power)
 
 
-def second_pass(power, first):
+def second_pass(power, first, grads):
     square = first.shape
     return pl.pallas_call(
         second_pass_kernel,
-        out_shape=jax.ShapeDtypeStruct((2 * square[0], square[1]), F32),
-        in_specs=[IN_VMEM] * 3,
-        out_specs=IN_VMEM,
-        scratch_shapes=[pltpu.VMEM(square, F32)] * 2,
+        out_shape=(
+            jax.ShapeDtypeStruct((2 * square[0], square[1]), F32),
+            jax.ShapeDtypeStruct(grads.shape, grads.dtype),
+        ),
+        in_specs=[IN_VMEM] * 3 + [IN_HBM],
+        out_specs=(IN_VMEM, IN_VMEM),
+        scratch_shapes=[pltpu.VMEM(square, F32)] * 2 + [pltpu.SemaphoreType.DMA],
         compiler_params=pltpu.CompilerParams(vmem_limit_bytes=32 << 20),
         cost_estimate=QR_COST,
-    )(*power, first)
+    )(*power, first, in_hbm(grads))
 
 
 def power_by_merged(power, grads, errors):
@@ -193,19 +242,21 @@
     return products[:rank, :] + products[rank:, :]
 
 
-def kept_factor_kernel(half_ref, grads_ref, errors_ref, power_ref, terms_ref, other_ref, held_g, held_e, sems, other_sem):
+def kept_factor_kernel(half_ref, grads_ref, errors_ref, power_ref, terms_ref, other_ref, own_e, sem, other_sem):
     count = power_ref.shape[0]
-    wait = load((grads_ref, errors_ref), (held_g, held_e), sems, [half_ref[0] * count], count)
-    rows = pl.ds(pl.multiple_of((1 - half_ref[0]) * count, count), count)
-    other = pltpu.make_async_copy(errors_ref.at[rows], other_ref, other_sem)
+    rows = half_rows(half_ref[0], count)
+    own = pltpu.make_async_copy(errors_ref.at[rows], own_e, sem)
+    other = pltpu.make_async_copy(errors_ref.at[half_rows(1 - half_ref[0], count)], other_ref, other_sem)
+    own.start()
     other.start()
-    wait(0)
-    terms_ref[...] = power_by_merged(power_ref[...], held_g[...], held_e[...])
+    own.wait()
+    terms_ref[...] = power_by_merged(power_ref[...], grads_ref[rows, :], own_e[...])
     other.wait()
 
 
-def other_factor_kernel(grads_ref, errors_ref, power_ref, before_ref, terms_ref):
-    terms_ref[...] = before_ref[...] + power_by_merged(power_ref[...], grads_ref[...], errors_ref[...])
+def other_factor_kernel(half_ref, grads_ref, errors_ref, power_ref, before_ref, terms_ref):
+    rows = half_rows(1 - half_ref[0], power_ref.shape[0])
+    terms_ref[...] = before_ref[...] + power_by_merged(power_ref[...], grads_ref[rows, :], errors_ref[...])
 
 
 def kept_factor_terms(grads, errors, power, half):
@@ -214,33 +265,33 @@
     return pl.pallas_call(
         kept_factor_kernel,
         out_shape=(jax.ShapeDtypeStruct((rank, cols), F32), jax.ShapeDtypeStruct((rows, cols), BF16)),
-        in_specs=[IN_SMEM, IN_HBM, IN_HBM, IN_VMEM],
+        in_specs=[IN_SMEM, IN_VMEM, IN_HBM, IN_VMEM],
         out_specs=(IN_VMEM, IN_VMEM),
-        scratch_shapes=[pltpu.VMEM((rows, cols), BF16)] * 2 + [pltpu.SemaphoreType.DMA((1, 2)), pltpu.SemaphoreType.DMA],
+        scratch_shapes=[pltpu.VMEM((rows, cols), BF16), pltpu.SemaphoreType.DMA, pltpu.SemaphoreType.DMA],
         compiler_params=pltpu.CompilerParams(vmem_limit_bytes=32 << 20),
         cost_estimate=HALF_COST,
-    )(half, in_hbm(grads), in_hbm(errors), power)
-
-
-def other_factor_terms(grads, errors, power, before):
+    )(half, grads, in_hbm(errors), power)
+
+
+def other_factor_terms(grads, other_errors, power, before, half):
     return pl.pallas_call(
         other_factor_kernel,
         out_shape=jax.ShapeDtypeStruct(before.shape, F32),
-        in_specs=[IN_VMEM] * 4,
+        in_specs=[IN_SMEM] + [IN_VMEM] * 4,
         out_specs=IN_VMEM,
         compiler_params=pltpu.CompilerParams(vmem_limit_bytes=32 << 20),
         cost_estimate=HALF_COST,
-    )(grads, errors, power, before)
+    )(half, grads, other_errors, power, before)
 
 
 def output_kernel(replicas, place_ref, grads_ref, errors_ref, kept_ref, other_ref, maps_ref, terms_ref,
-                  avg_ref, new_ref, q_ref, held_g, held_e, held_new, held_avg, held_q, sems, out_sems, avg_sem, q_sem):
+                  avg_ref, new_ref, q_ref, held_e, held_new, held_avg, held_q, sems, out_sems, avg_sem, q_sem):
     rank = kept_ref.shape[1]
     count = kept_ref.shape[0]
     share = avg_ref.shape[0]
     kept_half, own = place_ref[0], place_ref[1]
     starts = [kept_half * count, (1 - kept_half) * count]
-    wait = load((grads_ref, errors_ref), (held_g, held_e), sems, starts, count)
+    wait = load((errors_ref,), (held_e,), sems, starts, count)
     writes = []
 
     def write(held, out, sem):
@@ -263,7 +314,7 @@
     for k, power_ref in enumerate((kept_ref, other_ref)):
         wait(k)
         rows = slice(k * count, (k + 1) * count)
-        merged = held_g[rows, :].astype(F32) + held_e[rows, :].astype(F32)
+        merged = grads_ref[pl.ds(pl.multiple_of(starts[k], count), count), :].astype(F32) + held_e[rows, :].astype(F32)
         held_new[rows, :] = (merged - product(power_ref[...], mapped)).astype(BF16)
         out = pl.ds(pl.multiple_of(starts[k], count), count)
         write(held_new.at[pl.ds(k * count, count)], new_ref.at[out], out_sems.at[k])
@@ -285,7 +336,7 @@
     share = rows // replicas
     return pl.pallas_call(
         functools.partial(output_kernel, replicas),
-        in_specs=[IN_SMEM, IN_HBM, IN_HBM] + [IN_VMEM] * 4,
+        in_specs=[IN_SMEM, IN_VMEM, IN_HBM] + [IN_VMEM] * 4,
         out_specs=(IN_HBM, IN_HBM, IN_HBM),
         out_shape=(
             jax.ShapeDtypeStruct((share, cols), BF16),
@@ -295,16 +346,15 @@
         scratch_shapes=[
             pltpu.VMEM((rows, cols), BF16),
             pltpu.VMEM((rows, cols), BF16),
-            pltpu.VMEM((rows, cols), BF16),
             pltpu.VMEM((share, cols), BF16),
             pltpu.VMEM((cols, rank), F32),
-            pltpu.SemaphoreType.DMA((2, 2)),
+            pltpu.SemaphoreType.DMA((2, 1)),
             pltpu.SemaphoreType.DMA((2,)),
             pltpu.SemaphoreType.DMA,
             pltpu.SemaphoreType.DMA,
         ],
-        compiler_params=pltpu.CompilerParams(vmem_limit_bytes=52 << 20),
-    )(place, in_hbm(grads), in_hbm(errors), *power, maps, terms)
+        compiler_params=pltpu.CompilerParams(vmem_limit_bytes=16 << 20),
+    )(place, grads, in_hbm(errors), *power, maps, terms)
 
 
 def exchange(values, axes, groups):
@@ -350,9 +400,9 @@
 def body(grads, errors, q_init):
     replicas = lax.axis_size(DP)
     half = lax.axis_index("core").reshape(1)
-    sent, other_grads = power_terms(grads, errors, q_init, 1 - half, keep=True)
+    sent, own_grads = sent_power_terms(grads, errors, q_init, half)
     received = swap(sent)
-    power = power_terms(grads, errors, q_init, half, keep=False) + received
+    power = kept_power_terms(own_grads, errors, q_init, half) + received
 
     near, far = z_groups(lax.axis_size("z"), 1)
     power = scatter_sum(power, ("y", "x"))
@@ -363,16 +413,16 @@
 
     near, far = z_groups(lax.axis_size("z"), lax.axis_size("y"))
     terms, other_errors = kept_factor_terms(grads, errors, power[0], half)
-    terms = other_factor_terms(other_grads, other_errors, power[1], terms)
+    terms = other_factor_terms(grads, other_errors, power[1], terms, half)
     first = first_pass(power)
     place = jnp.concatenate([half, lax.axis_index(DP).reshape(1)])
     terms = scatter_sum(terms, DP, near)
     terms, first, place = lax.optimization_barrier((terms, first, place))
     terms = exchange_sum(terms, DP, far)
     terms, first = lax.optimization_barrier((terms, first))
-    maps = second_pass(power, first)
+    maps, held_grads = second_pass(power, first, grads)
     terms = gather(terms, DP, near)
-    return outputs(grads, errors, power, maps, terms, replicas, place)
+    return outputs(held_grads, errors, power, maps, terms, replicas, place)
 
 
 def solution(mesh):

time: 127 us -> 126 us (level)
  the two profiles are of different devices: /device:TPU:2 before, /device:TPU:8 now
where the time goes in v7:
time: 126 us
  blocking collectives  79.1 us (63%)
  Pallas kernels  23.5 us (19%)
  starting transfers between devices  15.1 us (12%)
  waiting for transfers between devices  6.05 us (5%)
    all_to_all x5, blocking collectives, exchange(): lax.all_to_all(values, axes, 0, 0, axis_index_groups=groups, tiled=True)  79.1 us
    all_to_all x2, starting transfers between devices, exchange(): lax.all_to_all(values, axes, 0, 0, axis_index_groups=groups, tiled=True)  11.3 us
    pallas_call x1, Pallas kernels, second_pass(): pl.pallas_call(second_pass_kernel, out_shape=(jax.ShapeDtypeStruct((2 * s...  6.83 us
    all_to_all x2, waiting for transfers between devices, exchange(): lax.all_to_all(values, axes, 0, 0, axis_index_groups=groups, tiled=True)  5.98 us
    pallas_call x1, Pallas kernels, first_pass(): pl.pallas_call(first_pass_kernel, out_shape=jax.ShapeDtypeStruct(square,...  4.43 us
    pallas_call x1, Pallas kernels, outputs(): pl.pallas_call(functools.partial(output_kernel, replicas), in_specs=[IN_S...  4.11 us
    ppermute x2, starting transfers between devices, swap(): return lax.ppermute(values, 'core', [(0, 1), (1, 0)])  3.83 us
    pallas_call x1, Pallas kernels, sent_power_terms(): pl.pallas_call(sent_power_kernel, out_shape=(jax.ShapeDtypeStruct((rows,...  2.88 us
  transfers between devices with their start and end apart: 4, of which 3 were waited for; matrix products, arithmetic and copies ran while one was open for 0% of the time, Pallas kernels for 12%

profile of v7, /device:TPU:8, one launch (start us, length us, event | category | flops | bytes accessed | tf_op | source)
XLA Modules:
  0.0 125.6 jit_solution(5796827777548824126)
XLA Ops:
  0.6 0.0 copy-start.1
  0.6 2.9 %shard_map.58 = (f32[1024,128]{1,0:T(8,128)S(1)}, bf16[1024,384]{1,0:T(8,128)(2,1)S(1)}) custom-call(s32[1]{0:T(128)} %bitcast.half_ref, bf16[2048,384]{1,0:T(8,128)(2,1)} %grads_ref.7, bf16[2048,384]{1,0:T(8,128)(2,1)} %errors_ref.7, f32[384,128]{1,0:T(8,128)} %q_ref.3), custom_call_target="tpu_custom_call" | custom-call | flops 1200000000 | bytes 2097152 | tf_op jit(solution)/shard_map/pallas_call | solution.py:108
  3.5 1.9 %collective-permute-start = (f32[1024,128]{1,0:T(8,128)S(1)}, f32[1024,128]{1,0:T(8,128)S(1)}, u32[]{:S(2)}, u32[]{:S(2)}) collective-permute-start(f32[1024,128]{1,0:T(8,128)S(1)} %get-tuple-element.15), channel_id=1, source_target_pairs={{0,1},{1,0},{2,3},{3,2},{4,5},{5,4},{6,7},{7,6},{8,9},{9,8},{10,11... | collective-permute-start | bytes 1572872 | tf_op jit(solution)/shard_map/ppermute | solution.py:397
  5.5 0.0 copy-done.1
  5.5 2.1 %shard_map.59 = f32[1024,128]{1,0:T(8,128)S(1)} custom-call(s32[1]{0:T(128)} %bitcast.half_ref, bf16[1024,384]{1,0:T(8,128)(2,1)S(1)} %get-tuple-element.14.grads_ref, bf16[2048,384]{1,0:T(8,128)(2,1)} %errors_ref.7, f32[384,128]{1,0:T(8,128)S(1)} %copy-done.1), custom_call_target="tpu_custom_call" | custom-call | flops 1200000000 | bytes 2097152 | tf_op jit(solution)/shard_map/pallas_call | solution.py:130
  7.6 0.0 collective-permute-done
  7.6 0.1 add.6
  7.7 18.2 %all_to_all.52 = f32[16,64,128]{2,1,0:T(8,128)S(1)} all-to-all(f32[16,64,128]{2,1,0:T(8,128)S(1)} %bitcast.12), channel_id=1, replica_groups=mesh['z'=16,'y'=4,'x'=4,'core'=2] {'y','x'}, dimensions={0} | all-to-all | bytes 1048576 | tf_op jit(solution)/shard_map/all_to_all | solution.py:361
  25.9 0.0 copy-start
  26.0 10.4 %all_to_all.53 = f32[4,64,128]{2,1,0:T(8,128)S(1)} all-to-all(f32[4,64,128]{2,1,0:T(8,128)S(1)} %broadcast_in_dim.10), channel_id=1, replica_groups={{0,32,64,96},{128,160,192,224},{320,352,256,288},{448,480,384,416},{1,3..., dimensions={0} | all-to-all | bytes 262144 | tf_op jit(solution)/shard_map/all_to_all | solution.py:361
  36.4 23.4 %all_to_all.54 = f32[4,64,128]{2,1,0:T(8,128)S(1)} all-to-all(f32[4,64,128]{2,1,0:T(8,128)S(1)} %broadcast_in_dim.11), channel_id=1, replica_groups={{0,128,320,448},{32,160,352,480},{64,192,256,384},{96,224,288,416},{1,1..., dimensions={0} | all-to-all | bytes 262144 | tf_op jit(solution)/shard_map/all_to_all | solution.py:361
  59.9 13.4 %all_to_all.55 = f32[16,64,128]{2,1,0:T(8,128)S(1)} all-to-all(f32[16,64,128]{2,1,0:T(8,128)S(1)} %broadcast_in_dim.12), channel_id=1, replica_groups=mesh['z'=16,'y'=4,'x'=4,'core'=2] {'y','x'}, dimensions={0} | all-to-all | bytes 1048576 | tf_op jit(solution)/shard_map/all_to_all | solution.py:361
  73.3 1.9 %collective-permute-start.1 = (f32[1024,128]{1,0:T(8,128)S(1)}, f32[1024,128]{1,0:T(8,128)S(1)}, u32[]{:S(2)}, u32[]{:S(2)}) collective-permute-start(f32[1024,128]{1,0:T(8,128)S(1)} %bitcast.6), channel_id=1, source_target_pairs={{0,1},{1,0},{2,3},{3,2},{4,5},{5,4},{6,7},{7,6},{8,9},{9,8},{10,11... | collective-permute-start | bytes 1572872 | tf_op jit(solution)/shard_map/ppermute | solution.py:397
  75.2 0.0 copy-done
  75.2 1.8 %shard_map.60 = (f32[128,384]{1,0:T(8,128)S(1)}, bf16[1024,384]{1,0:T(8,128)(2,1)S(1)}) custom-call(s32[1]{0:T(128)} %bitcast.half_ref, bf16[2048,384]{1,0:T(8,128)(2,1)S(1)} %copy-done, bf16[2048,384]{1,0:T(8,128)(2,1)} %errors_ref.7, f32[1024,128]{1,0:T(8,128)S(1)} %bitcast.7), custom_call_target="tpu_custom_call" | custom-call | flops 1200000000 | bytes 2097152 | tf_op jit(solution)/shard_map/pallas_call | solution.py:265
  77.0 0.1 collective-permute-done.1.power_ref.other_ref
  77.1 1.3 %shard_map.61 = f32[128,384]{1,0:T(8,128)} custom-call(s32[1]{0:T(128)} %bitcast.half_ref, bf16[2048,384]{1,0:T(8,128)(2,1)S(1)} %copy-done, bf16[1024,384]{1,0:T(8,128)(2,1)S(1)} %get-tuple-element.16.errors_ref, f32[1024,128]{1,0:T(8,128)S(1)} %collective-permute-done.1.power_ref.other_ref, f32[128,384]{1,0:T(8,128)S(1)} %get-tuple-element.17.before_ref), custom_call_target="tpu_custom_call" | custom-call | flops 1200000000 | bytes 2097152 | tf_op jit(solution)/shard_map/pallas_call | solution.py:277
  78.4 5.5 %all-to-all-start.4 = ((f32[16,8,384]{2,1,0:T(8,128)}), f32[16,8,384]{2,1,0:T(8,128)S(1)}, u32[]{:S(2)}, u32[]{:S(2)}) async-start(f32[16,8,384]{2,1,0:T(8,128)} %bitcast.3), calls=%async_computation.4 | async-start | bytes 393216 | tf_op jit(solution)/shard_map/all_to_all | solution.py:361
  83.9 0.1 pad_add_fusion.place_ref
  84.0 4.4 %shard_map.62.first_ref = f32[128,128]{1,0:T(8,128)S(1)} custom-call(f32[1024,128]{1,0:T(8,128)S(1)} %bitcast.8, f32[1024,128]{1,0:T(8,128)S(1)} %collective-permute-done.1.power_ref.other_ref), custom_call_target="tpu_custom_call" | custom-call | flops 7000000000 | bytes 1048576 | tf_op jit(solution)/shard_map/pallas_call | solution.py:209
  88.4 4.7 %all-to-all-done.4 = f32[16,8,384]{2,1,0:T(8,128)S(1)} async-done(((f32[16,8,384]{2,1,0:T(8,128)}), f32[16,8,384]{2,1,0:T(8,128)S(1)}, u32[]{:S(2)}, u32[]{:S(2)}) %all-to-all-start.4) | async-done | bytes 196640 | tf_op jit(solution)/shard_map/all_to_all | solution.py:361
  93.2 13.6 %all_to_all.56 = f32[4,8,384]{2,1,0:T(8,128)S(1)} all-to-all(f32[4,8,384]{2,1,0:T(8,128)S(1)} %broadcast_in_dim.13), channel_id=1, replica_groups={{0,128,320,448},{8,136,328,456},{16,144,336,464},{24,152,344,472},{32,1..., dimensions={0} | all-to-all | bytes 98304 | tf_op jit(solution)/shard_map/all_to_all | solution.py:361
  106.8 0.7 broadcast_in_dim.14
  107.5 5.8 %all-to-all-start.6 = ((f32[16,8,384]{2,1,0:T(8,128)}), f32[16,8,384]{2,1,0:T(8,128)S(1)}, u32[]{:S(2)}, u32[]{:S(2)}) async-start(f32[16,8,384]{2,1,0:T(8,128)} %broadcast_in_dim.14), calls=%async_computation.6 | async-start | bytes 393216 | tf_op jit(solution)/shard_map/all_to_all | solution.py:361
  113.3 6.8 %shard_map.63 = (f32[256,128]{1,0:T(8,128)S(1)}, bf16[2048,384]{1,0:T(8,128)(2,1)S(1)}) custom-call(f32[1024,128]{1,0:T(8,128)S(1)} %bitcast.9, f32[1024,128]{1,0:T(8,128)S(1)} %collective-permute-done.1.power_ref.other_ref, f32[128,128]{1,0:T(8,128)S(1)} %shard_map.62.first_ref, bf16[2048,384]{1,0:T(8,128)(2,1)} %grads_ref.7), custom_call_target="tpu_custom_call" | custom-call | flops 7000000000 | bytes 1048576 | tf_op jit(solution)/shard_map/pallas_call | solution.py:222
  120.1 1.3 all-to-all-done.6
  121.4 4.1 %shard_map.64 = (bf16[32,384]{1,0:T(8,128)(2,1)}, bf16[2048,384]{1,0:T(8,128)(2,1)}, f32[384,128]{1,0:T(8,128)}) custom-call(s32[2]{0:T(128)S(1)} %pad_add_fusion.place_ref, bf16[2048,384]{1,0:T(8,128)(2,1)S(1)} %get-tuple-element.22.grads_ref, bf16[2048,384]{1,0:T(8,128)(2,1)} %errors_ref.7, f32[1024,128]{1,0:T(8,128)S(1)} %bitcast.10, ...), custom_call_target="tpu_custom_call" | custom-call | tf_op jit(solution)/shard_map/pallas_call | solution.py:337
  (9 shorter events, 0.2 us)
Async XLA Ops:
  0.6 4.8 %copy-start.1 = (f32[384,128]{1,0:T(8,128)S(1)}, f32[384,128]{1,0:T(8,128)}, u32[]{:S(2)}) copy-start(f32[384,128]{1,0:T(8,128)} %q_ref.3) | copy-start | bytes 589828
  3.5 4.1 %collective-permute-start = (f32[1024,128]{1,0:T(8,128)S(1)}, f32[1024,128]{1,0:T(8,128)S(1)}, u32[]{:S(2)}, u32[]{:S(2)}) collective-permute-start(f32[1024,128]{1,0:T(8,128)S(1)} %get-tuple-element.15), channel_id=1, source_target_pairs={{0,1},{1,0},{2,3},{3,2},{4,5},{5,4},{6,7},{7,6},{8,9},{9,8},{10,11... | collective-permute-start | bytes 1572872 | tf_op jit(solution)/shard_map/ppermute | solution.py:397
  25.9 49.3 %copy-start = (bf16[2048,384]{1,0:T(8,128)(2,1)S(1)}, bf16[2048,384]{1,0:T(8,128)(2,1)}, u32[]{:S(2)}) copy-start(bf16[2048,384]{1,0:T(8,128)(2,1)} %grads_ref.7) | copy-start | bytes 4718596
  73.3 3.8 %collective-permute-start.1 = (f32[1024,128]{1,0:T(8,128)S(1)}, f32[1024,128]{1,0:T(8,128)S(1)}, u32[]{:S(2)}, u32[]{:S(2)}) collective-permute-start(f32[1024,128]{1,0:T(8,128)S(1)} %bitcast.6), channel_id=1, source_target_pairs={{0,1},{1,0},{2,3},{3,2},{4,5},{5,4},{6,7},{7,6},{8,9},{9,8},{10,11... | collective-permute-start | bytes 1572872 | tf_op jit(solution)/shard_map/ppermute | solution.py:397
  78.4 14.8 %all-to-all-start.4 = ((f32[16,8,384]{2,1,0:T(8,128)}), f32[16,8,384]{2,1,0:T(8,128)S(1)}, u32[]{:S(2)}, u32[]{:S(2)}) async-start(f32[16,8,384]{2,1,0:T(8,128)} %bitcast.3), calls=%async_computation.4 | async-start | bytes 393216 | tf_op jit(solution)/shard_map/all_to_all | solution.py:361
  107.5 13.8 %all-to-all-start.6 = ((f32[16,8,384]{2,1,0:T(8,128)}), f32[16,8,384]{2,1,0:T(8,128)S(1)}, u32[]{:S(2)}, u32[]{:S(2)}) async-start(f32[16,8,384]{2,1,0:T(8,128)} %broadcast_in_dim.14), calls=%async_computation.6 | async-start | bytes 393216 | tf_op jit(solution)/shard_map/all_to_all | solution.py:361

commit v8 on v7

--- a/solution.py
+++ b/solution.py
@@ -14,6 +14,7 @@
 LANES_BY_LANES = (((1,), (1,)), ((), ()))
 WIDTH = 16
 CHUNK = 512
+PIECES = 2
 VMEM_BYTES = 16 << 20
 QR_COST = pl.CostEstimate(flops=7_000_000_000, bytes_accessed=1 << 20, transcendentals=0)
 
@@ -313,11 +314,14 @@
     mapped = right(product(maps_ref[rank:, :], terms))
     for k, power_ref in enumerate((kept_ref, other_ref)):
         wait(k)
-        rows = slice(k * count, (k + 1) * count)
-        merged = grads_ref[pl.ds(pl.multiple_of(starts[k], count), count), :].astype(F32) + held_e[rows, :].astype(F32)
-        held_new[rows, :] = (merged - product(power_ref[...], mapped)).astype(BF16)
-        out = pl.ds(pl.multiple_of(starts[k], count), count)
-        write(held_new.at[pl.ds(k * count, count)], new_ref.at[out], out_sems.at[k])
+        for part in range(PIECES):
+            size = count // PIECES
+            piece = slice(part * size, (part + 1) * size)
+            held = pl.ds(k * count + part * size, size)
+            rows = pl.ds(pl.multiple_of(starts[k] + part * size, size), size)
+            merged = grads_ref[rows, :].astype(F32) + held_e[held, :].astype(F32)
+            held_new[held, :] = (merged - product(power_ref[piece, :], mapped)).astype(BF16)
+            write(held_new.at[held], new_ref.at[rows], out_sems.at[k * PIECES + part])
         if k == 0:
             per_half = count // share
             rows = pl.ds(pl.multiple_of(lax.rem(own, per_half) * share, share), share)
@@ -349,7 +353,7 @@
             pltpu.VMEM((share, cols), BF16),
             pltpu.VMEM((cols, rank), F32),
             pltpu.SemaphoreType.DMA((2, 1)),
-            pltpu.SemaphoreType.DMA((2,)),
+            pltpu.SemaphoreType.DMA((2 * PIECES,)),
             pltpu.SemaphoreType.DMA,
             pltpu.SemaphoreType.DMA,
         ],

time: 126 us -> 126 us (level)
  no operation moved by 1% of the time
where the time goes in v8:
time: 126 us
  blocking collectives  79.1 us (63%)
  Pallas kernels  23.4 us (19%)
  starting transfers between devices  15.1 us (12%)
  waiting for transfers between devices  6.05 us (5%)
    all_to_all x5, blocking collectives, exchange(): lax.all_to_all(values, axes, 0, 0, axis_index_groups=groups, tiled=True)  79.1 us
    all_to_all x2, starting transfers between devices, exchange(): lax.all_to_all(values, axes, 0, 0, axis_index_groups=groups, tiled=True)  11.3 us
    pallas_call x1, Pallas kernels, second_pass(): pl.pallas_call(second_pass_kernel, out_shape=(jax.ShapeDtypeStruct((2 * s...  6.83 us
    all_to_all x2, waiting for transfers between devices, exchange(): lax.all_to_all(values, axes, 0, 0, axis_index_groups=groups, tiled=True)  5.98 us
    pallas_call x1, Pallas kernels, first_pass(): pl.pallas_call(first_pass_kernel, out_shape=jax.ShapeDtypeStruct(square,...  4.43 us
    pallas_call x1, Pallas kernels, outputs(): pl.pallas_call(functools.partial(output_kernel, replicas), in_specs=[IN_S...  4.02 us
    ppermute x2, starting transfers between devices, swap(): return lax.ppermute(values, 'core', [(0, 1), (1, 0)])  3.83 us
    pallas_call x1, Pallas kernels, sent_power_terms(): pl.pallas_call(sent_power_kernel, out_shape=(jax.ShapeDtypeStruct((rows,...  2.88 us
  transfers between devices with their start and end apart: 4, of which 3 were waited for; matrix products, arithmetic and copies ran while one was open for 0% of the time, Pallas kernels for 12%

profile of v8, /device:TPU:8, one launch (start us, length us, event | category | flops | bytes accessed | tf_op | source)
XLA Modules:
  0.0 125.6 jit_solution(13903382565825105281)
XLA Ops:
  0.6 0.0 copy-start.1
  0.6 2.9 %shard_map.58 = (f32[1024,128]{1,0:T(8,128)S(1)}, bf16[1024,384]{1,0:T(8,128)(2,1)S(1)}) custom-call(s32[1]{0:T(128)} %bitcast.half_ref, bf16[2048,384]{1,0:T(8,128)(2,1)} %grads_ref.7, bf16[2048,384]{1,0:T(8,128)(2,1)} %errors_ref.7, f32[384,128]{1,0:T(8,128)} %q_ref.3), custom_call_target="tpu_custom_call" | custom-call | flops 1200000000 | bytes 2097152 | tf_op jit(solution)/shard_map/pallas_call | solution.py:109
  3.5 1.9 %collective-permute-start = (f32[1024,128]{1,0:T(8,128)S(1)}, f32[1024,128]{1,0:T(8,128)S(1)}, u32[]{:S(2)}, u32[]{:S(2)}) collective-permute-start(f32[1024,128]{1,0:T(8,128)S(1)} %get-tuple-element.15), channel_id=1, source_target_pairs={{0,1},{1,0},{2,3},{3,2},{4,5},{5,4},{6,7},{7,6},{8,9},{9,8},{10,11... | collective-permute-start | bytes 1572872 | tf_op jit(solution)/shard_map/ppermute | solution.py:401
  5.5 0.0 copy-done.1
  5.5 2.1 %shard_map.59 = f32[1024,128]{1,0:T(8,128)S(1)} custom-call(s32[1]{0:T(128)} %bitcast.half_ref, bf16[1024,384]{1,0:T(8,128)(2,1)S(1)} %get-tuple-element.14.grads_ref, bf16[2048,384]{1,0:T(8,128)(2,1)} %errors_ref.7, f32[384,128]{1,0:T(8,128)S(1)} %copy-done.1), custom_call_target="tpu_custom_call" | custom-call | flops 1200000000 | bytes 2097152 | tf_op jit(solution)/shard_map/pallas_call | solution.py:131
  7.6 0.0 collective-permute-done
  7.6 0.1 add.6
  7.7 18.2 %all_to_all.52 = f32[16,64,128]{2,1,0:T(8,128)S(1)} all-to-all(f32[16,64,128]{2,1,0:T(8,128)S(1)} %bitcast.12), channel_id=1, replica_groups=mesh['z'=16,'y'=4,'x'=4,'core'=2] {'y','x'}, dimensions={0} | all-to-all | bytes 1048576 | tf_op jit(solution)/shard_map/all_to_all | solution.py:365
  25.9 0.0 copy-start
  26.0 10.4 %all_to_all.53 = f32[4,64,128]{2,1,0:T(8,128)S(1)} all-to-all(f32[4,64,128]{2,1,0:T(8,128)S(1)} %broadcast_in_dim.10), channel_id=1, replica_groups={{0,32,64,96},{128,160,192,224},{320,352,256,288},{448,480,384,416},{1,3..., dimensions={0} | all-to-all | bytes 262144 | tf_op jit(solution)/shard_map/all_to_all | solution.py:365
  36.4 23.4 %all_to_all.54 = f32[4,64,128]{2,1,0:T(8,128)S(1)} all-to-all(f32[4,64,128]{2,1,0:T(8,128)S(1)} %broadcast_in_dim.11), channel_id=1, replica_groups={{0,128,320,448},{32,160,352,480},{64,192,256,384},{96,224,288,416},{1,1..., dimensions={0} | all-to-all | bytes 262144 | tf_op jit(solution)/shard_map/all_to_all | solution.py:365
  59.9 13.4 %all_to_all.55 = f32[16,64,128]{2,1,0:T(8,128)S(1)} all-to-all(f32[16,64,128]{2,1,0:T(8,128)S(1)} %broadcast_in_dim.12), channel_id=1, replica_groups=mesh['z'=16,'y'=4,'x'=4,'core'=2] {'y','x'}, dimensions={0} | all-to-all | bytes 1048576 | tf_op jit(solution)/shard_map/all_to_all | solution.py:365
  73.3 1.9 %collective-permute-start.1 = (f32[1024,128]{1,0:T(8,128)S(1)}, f32[1024,128]{1,0:T(8,128)S(1)}, u32[]{:S(2)}, u32[]{:S(2)}) collective-permute-start(f32[1024,128]{1,0:T(8,128)S(1)} %bitcast.6), channel_id=1, source_target_pairs={{0,1},{1,0},{2,3},{3,2},{4,5},{5,4},{6,7},{7,6},{8,9},{9,8},{10,11... | collective-permute-start | bytes 1572872 | tf_op jit(solution)/shard_map/ppermute | solution.py:401
  75.2 0.0 copy-done
  75.2 1.8 %shard_map.60 = (f32[128,384]{1,0:T(8,128)S(1)}, bf16[1024,384]{1,0:T(8,128)(2,1)S(1)}) custom-call(s32[1]{0:T(128)} %bitcast.half_ref, bf16[2048,384]{1,0:T(8,128)(2,1)S(1)} %copy-done, bf16[2048,384]{1,0:T(8,128)(2,1)} %errors_ref.7, f32[1024,128]{1,0:T(8,128)S(1)} %bitcast.7), custom_call_target="tpu_custom_call" | custom-call | flops 1200000000 | bytes 2097152 | tf_op jit(solution)/shard_map/pallas_call | solution.py:266
  77.0 0.1 collective-permute-done.1.power_ref.other_ref
  77.1 1.3 %shard_map.61 = f32[128,384]{1,0:T(8,128)} custom-call(s32[1]{0:T(128)} %bitcast.half_ref, bf16[2048,384]{1,0:T(8,128)(2,1)S(1)} %copy-done, bf16[1024,384]{1,0:T(8,128)(2,1)S(1)} %get-tuple-element.16.errors_ref, f32[1024,128]{1,0:T(8,128)S(1)} %collective-permute-done.1.power_ref.other_ref, f32[128,384]{1,0:T(8,128)S(1)} %get-tuple-element.17.before_ref), custom_call_target="tpu_custom_call" | custom-call | flops 1200000000 | bytes 2097152 | tf_op jit(solution)/shard_map/pallas_call | solution.py:278
  78.4 5.5 %all-to-all-start.4 = ((f32[16,8,384]{2,1,0:T(8,128)}), f32[16,8,384]{2,1,0:T(8,128)S(1)}, u32[]{:S(2)}, u32[]{:S(2)}) async-start(f32[16,8,384]{2,1,0:T(8,128)} %bitcast.3), calls=%async_computation.4 | async-start | bytes 393216 | tf_op jit(solution)/shard_map/all_to_all | solution.py:365
  83.9 0.1 pad_add_fusion.place_ref
  84.0 4.4 %shard_map.62.first_ref = f32[128,128]{1,0:T(8,128)S(1)} custom-call(f32[1024,128]{1,0:T(8,128)S(1)} %bitcast.8, f32[1024,128]{1,0:T(8,128)S(1)} %collective-permute-done.1.power_ref.other_ref), custom_call_target="tpu_custom_call" | custom-call | flops 7000000000 | bytes 1048576 | tf_op jit(solution)/shard_map/pallas_call | solution.py:210
  88.4 4.7 %all-to-all-done.4 = f32[16,8,384]{2,1,0:T(8,128)S(1)} async-done(((f32[16,8,384]{2,1,0:T(8,128)}), f32[16,8,384]{2,1,0:T(8,128)S(1)}, u32[]{:S(2)}, u32[]{:S(2)}) %all-to-all-start.4) | async-done | bytes 196640 | tf_op jit(solution)/shard_map/all_to_all | solution.py:365
  93.2 13.6 %all_to_all.56 = f32[4,8,384]{2,1,0:T(8,128)S(1)} all-to-all(f32[4,8,384]{2,1,0:T(8,128)S(1)} %broadcast_in_dim.13), channel_id=1, replica_groups={{0,128,320,448},{8,136,328,456},{16,144,336,464},{24,152,344,472},{32,1..., dimensions={0} | all-to-all | bytes 98304 | tf_op jit(solution)/shard_map/all_to_all | solution.py:365
  106.8 0.7 broadcast_in_dim.14
  107.5 5.8 %all-to-all-start.6 = ((f32[16,8,384]{2,1,0:T(8,128)}), f32[16,8,384]{2,1,0:T(8,128)S(1)}, u32[]{:S(2)}, u32[]{:S(2)}) async-start(f32[16,8,384]{2,1,0:T(8,128)} %broadcast_in_dim.14), calls=%async_computation.6 | async-start | bytes 393216 | tf_op jit(solution)/shard_map/all_to_all | solution.py:365
  113.3 6.8 %shard_map.63 = (f32[256,128]{1,0:T(8,128)S(1)}, bf16[2048,384]{1,0:T(8,128)(2,1)S(1)}) custom-call(f32[1024,128]{1,0:T(8,128)S(1)} %bitcast.9, f32[1024,128]{1,0:T(8,128)S(1)} %collective-permute-done.1.power_ref.other_ref, f32[128,128]{1,0:T(8,128)S(1)} %shard_map.62.first_ref, bf16[2048,384]{1,0:T(8,128)(2,1)} %grads_ref.7), custom_call_target="tpu_custom_call" | custom-call | flops 7000000000 | bytes 1048576 | tf_op jit(solution)/shard_map/pallas_call | solution.py:223
  120.1 1.3 all-to-all-done.6
  121.4 4.0 %shard_map.64 = (bf16[32,384]{1,0:T(8,128)(2,1)}, bf16[2048,384]{1,0:T(8,128)(2,1)}, f32[384,128]{1,0:T(8,128)}) custom-call(s32[2]{0:T(128)S(1)} %pad_add_fusion.place_ref, bf16[2048,384]{1,0:T(8,128)(2,1)S(1)} %get-tuple-element.22.grads_ref, bf16[2048,384]{1,0:T(8,128)(2,1)} %errors_ref.7, f32[1024,128]{1,0:T(8,128)S(1)} %bitcast.10, ...), custom_call_target="tpu_custom_call" | custom-call | tf_op jit(solution)/shard_map/pallas_call | solution.py:341
  (9 shorter events, 0.2 us)
Async XLA Ops:
  0.6 4.8 %copy-start.1 = (f32[384,128]{1,0:T(8,128)S(1)}, f32[384,128]{1,0:T(8,128)}, u32[]{:S(2)}) copy-start(f32[384,128]{1,0:T(8,128)} %q_ref.3) | copy-start | bytes 589828
  3.5 4.1 %collective-permute-start = (f32[1024,128]{1,0:T(8,128)S(1)}, f32[1024,128]{1,0:T(8,128)S(1)}, u32[]{:S(2)}, u32[]{:S(2)}) collective-permute-start(f32[1024,128]{1,0:T(8,128)S(1)} %get-tuple-element.15), channel_id=1, source_target_pairs={{0,1},{1,0},{2,3},{3,2},{4,5},{5,4},{6,7},{7,6},{8,9},{9,8},{10,11... | collective-permute-start | bytes 1572872 | tf_op jit(solution)/shard_map/ppermute | solution.py:401
  25.9 49.3 %copy-start = (bf16[2048,384]{1,0:T(8,128)(2,1)S(1)}, bf16[2048,384]{1,0:T(8,128)(2,1)}, u32[]{:S(2)}) copy-start(bf16[2048,384]{1,0:T(8,128)(2,1)} %grads_ref.7) | copy-start | bytes 4718596
  73.3 3.8 %collective-permute-start.1 = (f32[1024,128]{1,0:T(8,128)S(1)}, f32[1024,128]{1,0:T(8,128)S(1)}, u32[]{:S(2)}, u32[]{:S(2)}) collective-permute-start(f32[1024,128]{1,0:T(8,128)S(1)} %bitcast.6), channel_id=1, source_target_pairs={{0,1},{1,0},{2,3},{3,2},{4,5},{5,4},{6,7},{7,6},{8,9},{9,8},{10,11... | collective-permute-start | bytes 1572872 | tf_op jit(solution)/shard_map/ppermute | solution.py:401
  78.4 14.8 %all-to-all-start.4 = ((f32[16,8,384]{2,1,0:T(8,128)}), f32[16,8,384]{2,1,0:T(8,128)S(1)}, u32[]{:S(2)}, u32[]{:S(2)}) async-start(f32[16,8,384]{2,1,0:T(8,128)} %bitcast.3), calls=%async_computation.4 | async-start | bytes 393216 | tf_op jit(solution)/shard_map/all_to_all | solution.py:365
  107.5 13.8 %all-to-all-start.6 = ((f32[16,8,384]{2,1,0:T(8,128)}), f32[16,8,384]{2,1,0:T(8,128)S(1)}, u32[]{:S(2)}, u32[]{:S(2)}) async-start(f32[16,8,384]{2,1,0:T(8,128)} %broadcast_in_dim.14), calls=%async_computation.6 | async-start | bytes 393216 | tf_op jit(solution)/shard_map/all_to_all | solution.py:365
